TPU v7x, 32 devices: a whole 2x2x4 slice. The times are simulated.
32 devices in a mesh: section: 2 (over core), ctx: 4 (over y, x), tensor: 4 (over z).
Axes of the slice: x: 2, y: 2, z: 4, core: 2. Of those that a mesh axis runs over, the one named last changes fastest.
Arguments:
- block_input: bfloat16 [2, 1024, 2048], P(None, 'ctx', 'tensor'), may hold values from -6 to 6
- out_cotangent: bfloat16 [2, 1024, 2048], P(None, 'ctx', 'tensor'), may hold values from -6 to 6
- doc_lengths: int32 [2, 6], replicated, may hold values from 200 to 2000, as said below
- norm_gain: bfloat16 [2, 2, 2048], P('section', None, 'tensor'), may hold values from 0.5 to 1.5
- norm_bias: bfloat16 [2, 2, 2048], P('section', None, 'tensor'), may hold values from -3 to 3
- qkv_weight: bfloat16 [2, 2048, 3, 2048], P('section', 'ctx', None, 'tensor'), may hold values from -0.125 to 0.125
- qkv_bias: bfloat16 [2, 3, 2048], P('section', None, 'tensor'), may hold values from -3 to 3
- out_weight: bfloat16 [2, 2048, 2048], P('section', 'tensor', 'ctx'), may hold values from -0.25 to 0.25
- out_bias: bfloat16 [2, 2048], P('section', 'tensor'), may hold values from -3 to 3
- up_weight: bfloat16 [2, 2048, 8192], P('section', 'ctx', 'tensor'), may hold values from -0.125 to 0.125
- up_bias: bfloat16 [2, 8192], P('section', 'tensor'), may hold values from -3 to 3
- down_weight: bfloat16 [2, 8192, 2048], P('section', 'tensor', 'ctx'), may hold values from -0.0625 to 0.0625
- down_bias: bfloat16 [2, 2048], P('section', 'tensor'), may hold values from -3 to 3
Outputs:
- hidden_states: bfloat16 [2, 2, 1024, 2048], P('section', None, 'ctx', 'tensor')
- input_grads: bfloat16 [2, 2, 1024, 2048], P('section', None, 'ctx', 'tensor')
- norm_gain_grad: float32 [2, 2, 2048], P('section', None, 'tensor')
- norm_bias_grad: float32 [2, 2, 2048], P('section', None, 'tensor')
- qkv_weight_grad: float32 [2, 2048, 3, 2048], P('section', 'ctx', None, 'tensor')
- qkv_bias_grad: float32 [2, 3, 2048], P('section', None, 'tensor')
- out_weight_grad: float32 [2, 2048, 2048], P('section', 'tensor', 'ctx')
- out_bias_grad: float32 [2, 2048], P('section', 'tensor')
- up_weight_grad: float32 [2, 2048, 8192], P('section', 'ctx', 'tensor')
- up_bias_grad: float32 [2, 8192], P('section', 'tensor')
- down_weight_grad: float32 [2, 8192, 2048], P('section', 'tensor', 'ctx')
- down_bias_grad: float32 [2, 2048], P('section', 'tensor')
Inputs may be any that keep to these rules, and one draw needn't show every extreme that they name: `doc_lengths`: in each row, documents follow one another from position 0 with these lengths; the last ones may run past the sequence. In one micro-batch, drawn from the seed, the first length is 1024, so one document covers the whole sequence.
All inputs are finite; a program needn't handle non-finite values.
Results may differ from a plain program's by a relative error of at most 0.018.
Values may be sent and summed in bfloat16 or wider, within the bound.
No kernel may reach another device: no remote copies, remote signals or barrier semaphores. Data moves between devices by JAX's collectives and lax.ppermute only.
A program may use at most 256 MiB of HBM per device.

v0:
```python
import jax
import jax.numpy as jnp
from jax import lax
from jax.sharding import PartitionSpec as P

ROT = 64
HD = 256


EPSILON = 1e-05


def passed_along(value, axis, steps):
    count = lax.axis_size(axis)
    initial, last = (max(0, -steps), min(count, count - steps))
    return lax.ppermute(value, axis, [(source, source + steps) for source in range(initial, last)])


def doc_layout(lengths, positions):
    doc_ends = jnp.cumsum(lengths)
    passed = doc_ends[None, :] <= positions[:, None]
    segment = jnp.sum(passed.astype(jnp.int32), axis=1)
    begins = jnp.max(jnp.where(passed, doc_ends[None, :], 0), axis=1)
    return (segment, positions - begins)


def rotary_tables(positions, rot_dims):
    inverse = 10000.0 ** (-jnp.arange(0, rot_dims, 2, dtype=jnp.float32) / rot_dims)
    angles = positions.astype(jnp.float32)[:, None] * inverse[None, :]
    return (jnp.cos(angles)[:, None, :], jnp.sin(angles)[:, None, :])


def rotate(field, cosine_table, sine_table):
    half_rot = cosine_table.shape[-1]
    front_half = field[..., :half_rot]
    back_half = field[..., half_rot : 2 * half_rot]
    return jnp.concatenate(
        [
            front_half * cosine_table - back_half * sine_table,
            back_half * cosine_table + front_half * sine_table,
            field[..., 2 * half_rot :],
        ],
        axis=-1,
    )


def unrotate(grad_field, cosine_table, sine_table):
    half_rot = cosine_table.shape[-1]
    front_half = grad_field[..., :half_rot]
    back_half = grad_field[..., half_rot : 2 * half_rot]
    return jnp.concatenate(
        [
            front_half * cosine_table + back_half * sine_table,
            back_half * cosine_table - front_half * sine_table,
            grad_field[..., 2 * half_rot :],
        ],
        axis=-1,
    )


def normalize(values, gain_row, bias_row):
    centered = values - jnp.mean(values, axis=-1, keepdims=True)
    variance = jnp.mean(centered * centered, axis=-1, keepdims=True)
    inv_std = lax.rsqrt(variance + EPSILON)
    normed = centered * inv_std
    return (normed * gain_row + bias_row, normed, inv_std)


def norm_backward(grad_norm, normed, inv_std, gain_row):
    scaled = grad_norm * gain_row
    return inv_std * (
        scaled
        - jnp.mean(scaled, axis=-1, keepdims=True)
        - normed * jnp.mean(scaled * normed, axis=-1, keepdims=True)
    )


def gelu_exact(values):
    return jax.nn.gelu(values, approximate=False)


def pair_grads(
    queries,
    grad_rows,
    log_mass,
    row_delta,
    query_pos,
    query_seg,
    key_tile,
    value_tile,
    key_pos,
    key_seg,
    scaling,
):
    scores = (
        jnp.einsum("qhd,khd->qhk", queries, key_tile, preferred_element_type=jnp.float32) * scaling
    )
    allowed = ((key_pos[None, :] <= query_pos[:, None]) & (key_seg[None, :] == query_seg[:, None]))[
        :, None, :
    ]
    probability = jnp.where(allowed, jnp.exp(scores - log_mass[..., None]), 0.0)
    grad_prob = jnp.einsum(
        "qhd,khd->qhk", grad_rows, value_tile, preferred_element_type=jnp.float32
    )
    grad_score = (probability * (grad_prob - row_delta[..., None])).astype(jnp.bfloat16)
    grad_query = None
    grad_key = None
    grad_value = None
    grad_query = (
        jnp.einsum("qhk,khd->qhd", grad_score, key_tile, preferred_element_type=jnp.float32)
        * scaling
    )
    grad_key = (
        jnp.einsum("qhk,qhd->khd", grad_score, queries, preferred_element_type=jnp.float32)
        * scaling
    )
    grad_value = jnp.einsum(
        "qhk,qhd->khd",
        probability.astype(jnp.bfloat16),
        grad_rows,
        preferred_element_type=jnp.float32,
    )
    return (grad_query, grad_key, grad_value)


def put_slot(buffer, slot_id, is_valid, fresh):
    former = lax.dynamic_index_in_dim(buffer, slot_id, 0, keepdims=False)
    return lax.dynamic_update_index_in_dim(buffer, jnp.where(is_valid, fresh, former), slot_id, 0)


def shards(
    block_input,
    out_cotangent,
    doc_lengths,
    norm_gain,
    norm_bias,
    qkv_weight,
    qkv_bias,
    out_weight,
    out_bias,
    up_weight,
    up_bias,
    down_weight,
    down_bias,
):
    section_count = lax.axis_size("section")
    section_id = lax.axis_index("section")
    ctx_count = lax.axis_size("ctx")
    ctx_id = lax.axis_index("ctx")
    tensor_id = lax.axis_index("tensor")
    micro_count, row_count, shard_width = block_input.shape
    seq_len = row_count * ctx_count
    w_qkv, w_up, w_out, w_down = (
        lax.all_gather(qkv_weight[0], "ctx", axis=0, tiled=True),
        lax.all_gather(up_weight[0], "ctx", axis=0, tiled=True),
        lax.all_gather(out_weight[0], "ctx", axis=1, tiled=True),
        lax.all_gather(down_weight[0], "ctx", axis=1, tiled=True),
    )
    model_width = w_qkv.shape[0]
    local_width = w_qkv.shape[2]
    head_count = local_width // HD
    hidden = w_up.shape[1]
    w_qkv_flat = w_qkv.reshape(model_width, 3 * local_width)
    bias_qkv = qkv_bias[0].astype(jnp.float32).reshape(3 * local_width)
    bias_up = up_bias[0].astype(jnp.float32)
    bias_sum = out_bias[0].astype(jnp.float32) + down_bias[0].astype(jnp.float32)
    gain_local = norm_gain[0]
    bias_local = norm_bias[0]
    row_index = ctx_id * row_count + jnp.arange(row_count, dtype=jnp.int32)
    key_index = jnp.arange(seq_len, dtype=jnp.int32)
    scaling = HD ** (-0.5)
    group_size = ctx_count
    while group_size > 1 and (row_count * group_size > 2048 or ctx_count % group_size):
        group_size -= 1
    tile_rows = row_count * group_size
    tile_count = seq_len // tile_rows

    def layout(slot_id):
        lengths = lax.dynamic_index_in_dim(doc_lengths, slot_id, 0, keepdims=False)
        key_seg, key_pos = doc_layout(lengths, key_index)
        query_seg = lax.dynamic_slice_in_dim(key_seg, ctx_id * row_count, row_count)
        query_pos = lax.dynamic_slice_in_dim(key_pos, ctx_id * row_count, row_count)
        cosine_table, sine_table = rotary_tables(query_pos, ROT)
        return (key_seg, query_seg, cosine_table, sine_table)

    def prepare(gathered, gain_full, bias_full, cosine_table, sine_table):
        values = gathered.astype(jnp.float32)
        gains = gain_full.astype(jnp.float32)
        biases = bias_full.astype(jnp.float32)
        norm_one, normed_one, inv_one = normalize(values, gains[0], biases[0])
        norm_two, normed_two, inv_two = normalize(values, gains[1], biases[1])
        norm_one = norm_one.astype(jnp.bfloat16)
        norm_two = norm_two.astype(jnp.bfloat16)
        mixture = jnp.dot(norm_one, w_qkv_flat, preferred_element_type=jnp.float32) + bias_qkv
        mixture = mixture.reshape(row_count, 3, head_count, HD)
        queries = rotate(mixture[:, 0], cosine_table, sine_table).astype(jnp.bfloat16)
        keys_rot = rotate(mixture[:, 1], cosine_table, sine_table).astype(jnp.bfloat16)
        values_h = mixture[:, 2].astype(jnp.bfloat16)
        pre_up = jnp.dot(norm_two, w_up, preferred_element_type=jnp.float32) + bias_up
        return (
            norm_one,
            normed_one,
            inv_one,
            norm_two,
            normed_two,
            inv_two,
            gains,
            queries,
            keys_rot,
            values_h,
            pre_up,
        )

    tick_count = micro_count + section_count - 1
    received = jnp.zeros((row_count, shard_width), jnp.bfloat16)
    saved_inputs = jnp.zeros((micro_count, row_count, shard_width), jnp.bfloat16)
    saved_attn = jnp.zeros((micro_count, row_count, head_count, HD), jnp.float32)
    saved_mass = jnp.zeros((micro_count, row_count, head_count), jnp.float32)
    states = jnp.zeros((micro_count, row_count, shard_width), jnp.bfloat16)
    for tick_id in range(tick_count):
        slot_raw = tick_id - section_id
        is_valid = (slot_raw >= 0) & (slot_raw < micro_count)
        slot_id = jnp.clip(slot_raw, 0, micro_count - 1)
        layer_in = jnp.where(section_id == 0, block_input[min(tick_id, micro_count - 1)], received)
        forward_key_seg, forward_query_seg, forward_cosine_table, forward_sine_table = layout(
            slot_id
        )
        forward_gathered = lax.all_gather(layer_in, "tensor", axis=1, tiled=True)
        forward_gain_full = lax.all_gather(gain_local, "tensor", axis=1, tiled=True)
        forward_bias_full = lax.all_gather(bias_local, "tensor", axis=1, tiled=True)
        prepared = prepare(
            forward_gathered,
            forward_gain_full,
            forward_bias_full,
            forward_cosine_table,
            forward_sine_table,
        )
        forward_queries = prepared[7]
        forward_keys_rot = prepared[8]
        forward_values_h = prepared[9]
        forward_pre_up = prepared[10]
        running_max = jnp.full((row_count, head_count), -1e30, jnp.float32)
        attend_key_tile = lax.all_gather(forward_keys_rot, "ctx", axis=0, tiled=True)
        attend_value_tile = lax.all_gather(forward_values_h, "ctx", axis=0, tiled=True)
        key_count = attend_key_tile.shape[0]
        attend_key_pos = jnp.arange(key_count, dtype=jnp.int32)
        allowed = (
            (attend_key_pos[None, :] <= row_index[:, None])
            & (forward_key_seg[None, :] == forward_query_seg[:, None])
        )[:, None, :]
        scores = (
            jnp.einsum(
                "qhd,khd->qhk", forward_queries, attend_key_tile, preferred_element_type=jnp.float32
            )
            * scaling
        )
        new_max = jnp.maximum(running_max, jnp.max(jnp.where(allowed, scores, -1e30), axis=-1))
        weights_tile = jnp.where(allowed, jnp.exp(scores - new_max[..., None]), 0.0)
        running_sum = jnp.sum(weights_tile, axis=-1)
        weighted = jnp.einsum(
            "qhk,khd->qhd",
            weights_tile.astype(jnp.bfloat16),
            attend_value_tile,
            preferred_element_type=jnp.float32,
        )
        weighted, running_max, running_sum = (weighted, new_max, running_sum)
        forward_attn_f = weighted / running_sum[..., None]
        forward_log_mass = running_max + jnp.log(running_sum)
        forward_attn_r = forward_attn_f.reshape(row_count, local_width).astype(jnp.bfloat16)
        forward_activated = gelu_exact(forward_pre_up).astype(jnp.bfloat16)
        partial_out = jnp.dot(forward_attn_r, w_out, preferred_element_type=jnp.float32) + jnp.dot(
            forward_activated, w_down, preferred_element_type=jnp.float32
        )
        summed = lax.psum_scatter(
            partial_out.astype(jnp.bfloat16), "tensor", scatter_dimension=1, tiled=True
        ).astype(jnp.float32)
        result = layer_in.astype(jnp.float32) + summed + bias_sum
        result, attn_f, log_mass = (result.astype(jnp.bfloat16), forward_attn_f, forward_log_mass)
        saved_inputs = put_slot(saved_inputs, slot_id, is_valid, layer_in)
        saved_attn = put_slot(saved_attn, slot_id, is_valid, attn_f)
        saved_mass = put_slot(saved_mass, slot_id, is_valid, log_mass)
        states = put_slot(states, slot_id, is_valid, result)
        if tick_id + 1 < tick_count:
            received = passed_along(result, "section", 1)
    totals = (
        jnp.zeros((2, shard_width), jnp.float32),
        jnp.zeros((2, shard_width), jnp.float32),
        jnp.zeros((model_width, 3 * local_width), jnp.float32),
        jnp.zeros((3 * local_width,), jnp.float32),
        jnp.zeros((local_width, model_width), jnp.float32),
        jnp.zeros((shard_width,), jnp.float32),
        jnp.zeros((model_width, hidden), jnp.float32),
        jnp.zeros((hidden,), jnp.float32),
        jnp.zeros((hidden, model_width), jnp.float32),
    )
    received_grad = jnp.zeros((row_count, shard_width), jnp.bfloat16)
    grads_in = jnp.zeros((micro_count, row_count, shard_width), jnp.bfloat16)
    for tick_id in range(tick_count):
        slot_raw = tick_id - (section_count - 1 - section_id)
        is_valid = (slot_raw >= 0) & (slot_raw < micro_count)
        slot_id = jnp.clip(slot_raw, 0, micro_count - 1)
        grad_out = jnp.where(
            section_id == section_count - 1,
            out_cotangent[min(tick_id, micro_count - 1)],
            received_grad,
        )
        layer_in = lax.dynamic_index_in_dim(saved_inputs, slot_id, 0, keepdims=False)
        attn_f = lax.dynamic_index_in_dim(saved_attn, slot_id, 0, keepdims=False)
        log_mass = lax.dynamic_index_in_dim(saved_mass, slot_id, 0, keepdims=False)
        backward_key_seg, backward_query_seg, backward_cosine_table, backward_sine_table = layout(
            slot_id
        )
        backward_gathered = lax.all_gather(layer_in, "tensor", axis=1, tiled=True)
        grad_full = lax.all_gather(grad_out, "tensor", axis=1, tiled=True)
        backward_gain_full = lax.all_gather(gain_local, "tensor", axis=1, tiled=True)
        backward_bias_full = lax.all_gather(bias_local, "tensor", axis=1, tiled=True)
        (
            backward_norm_one,
            backward_normed_one,
            backward_inv_one,
            backward_norm_two,
            backward_normed_two,
            backward_inv_two,
            backward_gains,
            backward_queries,
            backward_keys_rot,
            backward_values_h,
            backward_pre_up,
        ) = prepare(
            backward_gathered,
            backward_gain_full,
            backward_bias_full,
            backward_cosine_table,
            backward_sine_table,
        )
        attn_r = attn_f.reshape(row_count, local_width).astype(jnp.bfloat16)
        activated_f, gelu_pullback = jax.vjp(gelu_exact, backward_pre_up)
        activated = activated_f.astype(jnp.bfloat16)
        backward_grad_w_out = jnp.dot(attn_r.T, grad_full, preferred_element_type=jnp.float32)
        backward_grad_w_down = jnp.dot(activated.T, grad_full, preferred_element_type=jnp.float32)
        backward_grad_b_out = jnp.sum(grad_out.astype(jnp.float32), axis=0)
        grad_attn = jnp.dot(grad_full, w_out.T, preferred_element_type=jnp.float32)
        grad_act = jnp.dot(grad_full, w_down.T, preferred_element_type=jnp.float32)
        grad_attn_r = grad_attn.astype(jnp.bfloat16).reshape(row_count, head_count, HD)
        grad_up = gelu_pullback(grad_act)[0].astype(jnp.bfloat16)
        backward_grad_w_up = jnp.dot(
            backward_norm_two.T, grad_up, preferred_element_type=jnp.float32
        )
        backward_grad_b_up = jnp.sum(grad_up.astype(jnp.float32), axis=0)
        grad_norm_two = jnp.dot(grad_up, w_up.T, preferred_element_type=jnp.float32)
        row_delta = jnp.sum(grad_attn_r.astype(jnp.float32) * attn_f, axis=-1)
        key_all = lax.all_gather(backward_keys_rot, "ctx", axis=0, tiled=True)
        value_all = lax.all_gather(backward_values_h, "ctx", axis=0, tiled=True)

        def over_keys(grad_query, tile_id):
            first_key = tile_id * tile_rows
            key_tile = lax.dynamic_slice_in_dim(key_all, first_key, tile_rows)
            value_tile = lax.dynamic_slice_in_dim(value_all, first_key, tile_rows)
            key_pos = first_key + jnp.arange(tile_rows, dtype=jnp.int32)
            key_tile_seg = lax.dynamic_slice_in_dim(backward_key_seg, first_key, tile_rows)
            part_query, part_key, part_value = pair_grads(
                backward_queries,
                grad_attn_r,
                log_mass,
                row_delta,
                row_index,
                backward_query_seg,
                key_tile,
                value_tile,
                key_pos,
                key_tile_seg,
                scaling,
            )
            return (grad_query + part_query, (part_key, part_value))

        backward_tiles = jnp.arange(tile_count, dtype=jnp.int32)
        zero_rows = jnp.zeros((row_count, head_count, HD), jnp.float32)
        grad_query, (tiles_key, tiles_value) = lax.scan(
            lambda c, t: over_keys(c, t), zero_rows, backward_tiles
        )
        grad_key = lax.psum_scatter(
            tiles_key.reshape(seq_len, head_count, HD).astype(jnp.bfloat16),
            "ctx",
            scatter_dimension=0,
            tiled=True,
        ).astype(jnp.float32)
        grad_value = lax.psum_scatter(
            tiles_value.reshape(seq_len, head_count, HD).astype(jnp.bfloat16),
            "ctx",
            scatter_dimension=0,
            tiled=True,
        ).astype(jnp.float32)
        grad_mixture = jnp.stack(
            [
                unrotate(grad_query, backward_cosine_table, backward_sine_table),
                unrotate(grad_key, backward_cosine_table, backward_sine_table),
                grad_value,
            ],
            axis=1,
        )
        grad_mixture = grad_mixture.reshape(row_count, 3 * local_width).astype(jnp.bfloat16)
        backward_grad_w_qkv = jnp.dot(
            backward_norm_one.T, grad_mixture, preferred_element_type=jnp.float32
        )
        backward_grad_b_qkv = jnp.sum(grad_mixture.astype(jnp.float32), axis=0)
        grad_norm_one = jnp.dot(grad_mixture, w_qkv_flat.T, preferred_element_type=jnp.float32)
        feature_start = tensor_id * shard_width
        whole_one = lax.psum(grad_norm_one.astype(jnp.bfloat16), "tensor").astype(jnp.float32)
        whole_two = lax.psum(grad_norm_two.astype(jnp.bfloat16), "tensor").astype(jnp.float32)
        grad_input = norm_backward(
            whole_one, backward_normed_one, backward_inv_one, backward_gains[0]
        ) + norm_backward(whole_two, backward_normed_two, backward_inv_two, backward_gains[1])
        grad_input = lax.dynamic_slice_in_dim(grad_input, feature_start, shard_width, 1)
        backward_gain_terms = jnp.stack(
            [
                jnp.sum(whole_one * backward_normed_one, axis=0),
                jnp.sum(whole_two * backward_normed_two, axis=0),
            ]
        )
        backward_bias_terms = jnp.stack([jnp.sum(whole_one, axis=0), jnp.sum(whole_two, axis=0)])
        backward_gain_terms = lax.dynamic_slice_in_dim(
            backward_gain_terms, feature_start, shard_width, 1
        )
        backward_bias_terms = lax.dynamic_slice_in_dim(
            backward_bias_terms, feature_start, shard_width, 1
        )
        result_grad = (grad_out.astype(jnp.float32) + grad_input).astype(jnp.bfloat16)
        terms = (
            backward_gain_terms,
            backward_bias_terms,
            backward_grad_w_qkv,
            backward_grad_b_qkv,
            backward_grad_w_out,
            backward_grad_b_out,
            backward_grad_w_up,
            backward_grad_b_up,
            backward_grad_w_down,
        )
        keep_mask = is_valid.astype(jnp.float32)
        totals = jax.tree.map(lambda a, g: a + keep_mask * g, totals, terms)
        grads_in = put_slot(grads_in, slot_id, is_valid, result_grad)
        if tick_id + 1 < tick_count:
            received_grad = passed_along(result_grad, "section", -1)
    (
        gain_terms,
        bias_terms,
        grad_w_qkv,
        grad_b_qkv,
        grad_w_out,
        grad_b_out,
        grad_w_up,
        grad_b_up,
        grad_w_down,
    ) = totals
    shard_qkv, shard_up, shard_out, shard_down = (
        lax.psum_scatter(
            grad_w_qkv.reshape(model_width, 3, local_width).astype(jnp.bfloat16),
            "ctx",
            scatter_dimension=0,
            tiled=True,
        ).astype(jnp.float32),
        lax.psum_scatter(
            grad_w_up.astype(jnp.bfloat16), "ctx", scatter_dimension=0, tiled=True
        ).astype(jnp.float32),
        lax.psum_scatter(
            grad_w_out.astype(jnp.bfloat16), "ctx", scatter_dimension=1, tiled=True
        ).astype(jnp.float32),
        lax.psum_scatter(
            grad_w_down.astype(jnp.bfloat16), "ctx", scatter_dimension=1, tiled=True
        ).astype(jnp.float32),
    )
    gain_sum, bias_sum_grad, qkv_bias_sum, up_bias_sum, out_bias_sum = lax.psum(
        (gain_terms, bias_terms, grad_b_qkv, grad_b_up, grad_b_out), "ctx"
    )
    return (
        states[None],
        grads_in[None],
        gain_sum[None],
        bias_sum_grad[None],
        shard_qkv[None],
        qkv_bias_sum.reshape(3, local_width)[None],
        shard_out[None],
        out_bias_sum[None],
        shard_up[None],
        up_bias_sum[None],
        shard_down[None],
        out_bias_sum[None],
    )


def solution(mesh):
    in_specs = (
        P(None, "ctx", "tensor"),
        P(None, "ctx", "tensor"),
        P(),
        P("section", None, "tensor"),
        P("section", None, "tensor"),
        P("section", "ctx", None, "tensor"),
        P("section", None, "tensor"),
        P("section", "tensor", "ctx"),
        P("section", "tensor"),
        P("section", "ctx", "tensor"),
        P("section", "tensor"),
        P("section", "tensor", "ctx"),
        P("section", "tensor"),
    )
    out_specs = (
        P("section", None, "ctx", "tensor"),
        P("section", None, "ctx", "tensor"),
        P("section", None, "tensor"),
        P("section", None, "tensor"),
        P("section", "ctx", None, "tensor"),
        P("section", None, "tensor"),
        P("section", "tensor", "ctx"),
        P("section", "tensor"),
        P("section", "ctx", "tensor"),
        P("section", "tensor"),
        P("section", "tensor", "ctx"),
        P("section", "tensor"),
    )
    return jax.shard_map(shards, mesh=mesh, in_specs=in_specs, out_specs=out_specs, check_vma=False)
```

profile of v0, /device:TPU:0, one launch (start us, length us, event | category | flops | bytes accessed | tf_op | source)
XLA Modules:
  0.0 1789.1 jit_solution(9061530521421475084)
XLA Ops:
  49.6 63.4 %all-gather.65.cloned.1.call-done = bf16[1,2048,3,512]{1,3,2,0:T(8,128)(2,1)} async-done(((bf16[1,512,3,512]{1,3,2,0:T(8,128)(2,1)}), bf16[1,2048,3,512]{1,3,2,0:T(8,128)(2,1)}) %all-gather.65.cloned.1.call-update) | async-done | bytes 6291472 | tf_op jit(solution)/shard_map/all_gather | solution.py:154
  130.9 20.1 %all-gather.43.cloned.1.call-done = bf16[1024,2,256]{2,0,1:T(8,128)(2,1)} async-done(((bf16[256,2,256]{2,0,1:T(8,128)(2,1)}), bf16[1024,2,256]{2,0,1:T(8,128)(2,1)}) %all-gather.43.cloned.1.call-update) | async-done | bytes 1048592 | tf_op jit(solution)/shard_map/all_gather | solution.py:243
  154.7 25.0 %all-gather.67.cloned.1.call-done = bf16[1024,1,2,256]{0,3,2,1:T(8,128)(2,1)} async-done(((bf16[256,1,2,256]{0,3,2,1:T(8,128)(2,1)}), bf16[1024,1,2,256]{0,3,2,1:T(8,128)(2,1)}) %all-gather.67.cloned.1.call-update) | async-done | bytes 1048592 | tf_op jit(solution)/shard_map/all_gather | solution.py:244
  183.1 85.8 %all-gather.73.cloned.1.call-done = bf16[1,2048,2048]{2,1,0:T(8,128)(2,1)} async-done(((bf16[1,2048,512]{2,1,0:T(8,128)(2,1)}), bf16[1,2048,2048]{2,1,0:T(8,128)(2,1)}) %all-gather.73.cloned.1.call-update) | async-done | bytes 8388624 | tf_op jit(solution)/shard_map/all_gather | solution.py:157
  269.0 89.3 %all-gather.71.cloned.1.call-done = bf16[1,2048,2048]{2,1,0:T(8,128)(2,1)} async-done(((bf16[1,512,2048]{2,1,0:T(8,128)(2,1)}), bf16[1,2048,2048]{2,1,0:T(8,128)(2,1)}) %all-gather.71.cloned.1.call-update) | async-done | bytes 8388624 | tf_op jit(solution)/shard_map/all_gather | solution.py:155
  373.6 21.8 %all-gather.69.cloned.1.call-done = bf16[1,512,2048]{2,1,0:T(8,128)(2,1)} async-done(((bf16[1,512,512]{2,1,0:T(8,128)(2,1)}), bf16[1,512,2048]{2,1,0:T(8,128)(2,1)}) %all-gather.69.cloned.1.call-update) | async-done | bytes 2097168 | tf_op jit(solution)/shard_map/all_gather | solution.py:156
  399.4 27.2 %reduce-scatter.14.cloned.1.call-done = bf16[256,512]{1,0:T(8,128)(2,1)} async-done(((bf16[256,2048]{1,0:T(8,128)(2,1)}), bf16[256,512]{1,0:T(8,128)(2,1)}) %reduce-scatter.14.cloned.1.call-update) | async-done | bytes 262160 | tf_op jit(solution)/shard_map/reduce_scatter | solution.py:274
  482.4 15.7 fusion.8
  505.0 24.2 %all-gather.75.cloned.1.call-done = bf16[1024,1,2,256]{0,3,2,1:T(8,128)(2,1)} async-done(((bf16[256,1,2,256]{0,3,2,1:T(8,128)(2,1)}), bf16[1024,1,2,256]{0,3,2,1:T(8,128)(2,1)}) %all-gather.75.cloned.1.call-update) | async-done | bytes 1048592 | tf_op jit(solution)/shard_map/all_gather | solution.py:244
  535.7 26.2 %reduce-scatter.16.cloned.1.call-done = bf16[256,512]{1,0:T(8,128)(2,1)} async-done(((bf16[256,2048]{1,0:T(8,128)(2,1)}), bf16[256,512]{1,0:T(8,128)(2,1)}) %reduce-scatter.16.cloned.1.call-update) | async-done | bytes 262160 | tf_op jit(solution)/shard_map/reduce_scatter | solution.py:274
  570.3 24.1 %all-gather.49.cloned.1.call-done = bf16[256,2048]{1,0:T(8,128)(2,1)} async-done(((bf16[256,512]{1,0:T(8,128)(2,1)}), bf16[256,2048]{1,0:T(8,128)(2,1)}) %all-gather.49.cloned.1.call-update) | async-done | bytes 1048592 | tf_op jit(solution)/shard_map/all_gather | solution.py:228
  685.6 23.7 %all-gather.77.cloned.1.call-done = bf16[1024,1,2,256]{0,3,2,1:T(8,128)(2,1)} async-done(((bf16[256,1,2,256]{0,3,2,1:T(8,128)(2,1)}), bf16[1024,1,2,256]{0,3,2,1:T(8,128)(2,1)}) %all-gather.77.cloned.1.call-update) | async-done | bytes 1048592 | tf_op jit(solution)/shard_map/all_gather | solution.py:244
  717.6 20.1 %all-gather.53.cloned.1.call-done = bf16[1024,2,256]{2,0,1:T(8,128)(2,1)} async-done(((bf16[256,2,256]{2,0,1:T(8,128)(2,1)}), bf16[1024,2,256]{2,0,1:T(8,128)(2,1)}) %all-gather.53.cloned.1.call-update) | async-done | bytes 1048592 | tf_op jit(solution)/shard_map/all_gather | solution.py:352
  741.1 25.7 %all-gather.81.cloned.1.call-done = bf16[1024,1,2,256]{3,0,2,1:T(8,128)(2,1)} async-done(((bf16[256,1,2,256]{3,0,2,1:T(8,128)(2,1)}), bf16[1024,1,2,256]{3,0,2,1:T(8,128)(2,1)}) %all-gather.81.cloned.1.call-update) | async-done | bytes 1048592 | tf_op jit(solution)/shard_map/all_gather | solution.py:353
  802.5 27.6 %reduce-scatter.22.cloned.1.call-done = bf16[256,2,256]{2,0,1:T(8,128)(2,1)} async-done(((bf16[1024,2,256]{2,0,1:T(8,128)(2,1)}), bf16[256,2,256]{2,0,1:T(8,128)(2,1)}) %reduce-scatter.22.cloned.1.call-update) | async-done | bytes 262160 | tf_op jit(solution)/shard_map/reduce_scatter | solution.py:387
  840.5 19.2 %all-gather.85.cloned.1.call-done = bf16[1,256,2048]{2,1,0:T(8,128)(2,1)} async-done(((bf16[1,256,512]{2,1,0:T(8,128)(2,1)}), bf16[1,256,2048]{2,1,0:T(8,128)(2,1)}) %all-gather.85.cloned.1.call-update) | async-done | bytes 1048592 | tf_op jit(solution)/shard_map/all_gather | solution.py:313
  876.3 73.5 %all-reduce.12.cloned.1.call-done = (bf16[256,2048]{1,0:T(8,128)(2,1)}, bf16[256,2048]{1,0:T(8,128)(2,1)}) async-done(((bf16[256,2048]{1,0:T(8,128)(2,1)}, bf16[256,2048]{1,0:T(8,128)(2,1)}), (bf16[256,2048]{1,0:T(8,128)(2,1)}, bf16[256,2048]{1,0:T(8,128)(2,1)})) %all-reduce.12.cloned.1.call-update) | async-done | bytes 2097168 | tf_op jit(solution)/shard_map/psum | solution.py:409
  981.3 26.1 %all-gather.57.cloned.1.call-done = bf16[256,2048]{1,0:T(8,128)(2,1)} async-done(((bf16[256,512]{1,0:T(8,128)(2,1)}), bf16[256,2048]{1,0:T(8,128)(2,1)}) %all-gather.57.cloned.1.call-update) | async-done | bytes 1048592 | tf_op jit(solution)/shard_map/all_gather | solution.py:314
  1010.9 25.2 %all-gather.87.cloned.1.call-done = bf16[1024,1,2,256]{3,0,2,1:T(8,128)(2,1)} async-done(((bf16[256,1,2,256]{3,0,2,1:T(8,128)(2,1)}), bf16[1024,1,2,256]{3,0,2,1:T(8,128)(2,1)}) %all-gather.87.cloned.1.call-update) | async-done | bytes 1048592 | tf_op jit(solution)/shard_map/all_gather | solution.py:353
  1070.8 28.4 %reduce-scatter.26.cloned.1.call-done = bf16[256,2,256]{2,0,1:T(8,128)(2,1)} async-done(((bf16[1024,2,256]{2,0,1:T(8,128)(2,1)}), bf16[256,2,256]{2,0,1:T(8,128)(2,1)}) %reduce-scatter.26.cloned.1.call-update) | async-done | bytes 262160 | tf_op jit(solution)/shard_map/reduce_scatter | solution.py:387
  1109.3 19.5 %all-gather.89.cloned.1.call-done = bf16[1,256,2048]{2,1,0:T(8,128)(2,1)} async-done(((bf16[1,256,512]{2,1,0:T(8,128)(2,1)}), bf16[1,256,2048]{2,1,0:T(8,128)(2,1)}) %all-gather.89.cloned.1.call-update) | async-done | bytes 1048592 | tf_op jit(solution)/shard_map/all_gather | solution.py:313
  1146.5 72.0 %all-reduce.10.cloned.1.call-done = (bf16[256,2048]{1,0:T(8,128)(2,1)}, bf16[256,2048]{1,0:T(8,128)(2,1)}) async-done(((bf16[256,2048]{1,0:T(8,128)(2,1)}, bf16[256,2048]{1,0:T(8,128)(2,1)}), (bf16[256,2048]{1,0:T(8,128)(2,1)}, bf16[256,2048]{1,0:T(8,128)(2,1)})) %all-reduce.10.cloned.1.call-update) | async-done | bytes 2097168 | tf_op jit(solution)/shard_map/psum | solution.py:409
  1249.9 26.1 %all-gather.61.cloned.1.call-done = bf16[256,2048]{1,0:T(8,128)(2,1)} async-done(((bf16[256,512]{1,0:T(8,128)(2,1)}), bf16[256,2048]{1,0:T(8,128)(2,1)}) %all-gather.61.cloned.1.call-update) | async-done | bytes 1048592 | tf_op jit(solution)/shard_map/all_gather | solution.py:314
  1279.5 24.9 %all-gather.91.cloned.1.call-done = bf16[1024,1,2,256]{3,0,2,1:T(8,128)(2,1)} async-done(((bf16[256,1,2,256]{3,0,2,1:T(8,128)(2,1)}), bf16[1024,1,2,256]{3,0,2,1:T(8,128)(2,1)}) %all-gather.91.cloned.1.call-update) | async-done | bytes 1048592 | tf_op jit(solution)/shard_map/all_gather | solution.py:353
  1313.0 15.8 fusion.6
  1444.0 16.1 add_convert_fusion.1
  1482.9 18.3 %add_convert_fusion = bf16[2048,2048]{1,0:T(8,128)(2,1)} fusion(f32[2048,2048]{1,0:T(8,128)} %fusion.236, f32[2048,2048]{1,0:T(8,128)} %fusion.235, bf16[256,2048]{1,0:T(8,128)(2,1)S(1)} %copy-done.55, f32[]{:T(128)S(6)} %convert_element_type.630, f32[]{:T(128)S(6)} %convert_element_type.629, f32[]{:T(128)S(6)} %convert_element_type.628, f32[256,2048]{1,0:T(8,128)} %fusion.45), kind=kOutput, calls=%fused_computation | convolution fusion | flops 2206728192 | bytes 45088780 | tf_op jit(solution)/shard_map/dot_general | solution.py:340
  1508.6 16.5 all-reduce.8.cloned.1.call-done
  1531.3 17.8 all-reduce
  1553.4 44.6 %reduce-scatter.32.cloned.1.call-done = bf16[512,3,512]{2,0,1:T(8,128)(2,1)} async-done(((bf16[2048,3,512]{2,0,1:T(8,128)(2,1)}), bf16[512,3,512]{2,0,1:T(8,128)(2,1)}) %reduce-scatter.32.cloned.1.call-update) | async-done | bytes 1572880 | tf_op jit(solution)/shard_map/reduce_scatter | solution.py:456
  1601.5 86.3 %reduce-scatter.36.cloned.1.call-done = bf16[512,2048]{1,0:T(8,128)(2,1)} async-done(((bf16[2048,2048]{1,0:T(8,128)(2,1)}), bf16[512,2048]{1,0:T(8,128)(2,1)}) %reduce-scatter.36.cloned.1.call-update) | async-done | bytes 2097168 | tf_op jit(solution)/shard_map/reduce_scatter | solution.py:462
  1691.9 85.3 %reduce-scatter.38.cloned.1.call-done = bf16[2048,512]{1,0:T(8,128)(2,1)} async-done(((bf16[2048,2048]{1,0:T(8,128)(2,1)}), bf16[2048,512]{1,0:T(8,128)(2,1)}) %reduce-scatter.38.cloned.1.call-update) | async-done | bytes 2097168 | tf_op jit(solution)/shard_map/reduce_scatter | solution.py:468
  (743 shorter events, 636.6 us)
Async XLA Ops:
  9.2 103.8 %all-gather.65.cloned.1.call-start = ((), (), s32[]{:S(2)}) async-start(), calls=%async_computation.37 | async-start | bytes 7864320 | tf_op jit(solution)/shard_map/all_gather | solution.py:154
  10.8 140.2 %all-gather.43.cloned.1.call-start = ((), (), s32[]{:S(2)}) async-start(), calls=%async_computation.13 | async-start | bytes 1310720 | tf_op jit(solution)/shard_map/all_gather | solution.py:243
  125.4 143.5 %all-gather.73.cloned.1.call-start = ((), (), s32[]{:S(2)}) async-start(), calls=%async_computation.41 | async-start | bytes 10485760 | tf_op jit(solution)/shard_map/all_gather | solution.py:157
  126.1 232.2 %all-gather.71.cloned.1.call-start = ((), (), s32[]{:S(2)}) async-start(), calls=%async_computation.40 | async-start | bytes 10485760 | tf_op jit(solution)/shard_map/all_gather | solution.py:155
  126.6 268.7 %all-gather.69.cloned.1.call-start = ((), (), s32[]{:S(2)}) async-start(), calls=%async_computation.39 | async-start | bytes 2621440 | tf_op jit(solution)/shard_map/all_gather | solution.py:156
  127.4 299.2 %reduce-scatter.14.cloned.1.call-start = ((), (), s32[]{:S(2)}) async-start(), calls=%async_computation.14 | async-start | bytes 1310720 | tf_op jit(solution)/shard_map/reduce_scatter | solution.py:274
  482.3 79.6 %reduce-scatter.16.cloned.1.call-start = ((), (), s32[]{:S(2)}) async-start(), calls=%async_computation.17 | async-start | bytes 1310720 | tf_op jit(solution)/shard_map/reduce_scatter | solution.py:274
  568.4 84.3 %all-gather.83.cloned.1.call-start = ((), (), s32[]{:S(2)}) async-start(), calls=%async_computation.46 | async-start | bytes 1310720 | tf_op jit(solution)/shard_map/all_gather | solution.py:314
  569.8 111.3 %all-gather.51.cloned.1.call-start = ((), (), s32[]{:S(2)}) async-start(), calls=%async_computation.19 | async-start | bytes 1310720 | tf_op jit(solution)/shard_map/all_gather | solution.py:243
  608.6 100.7 %all-gather.77.cloned.1.call-start = ((), (), s32[]{:S(2)}) async-start(), calls=%async_computation.43 | async-start | bytes 1310720 | tf_op jit(solution)/shard_map/all_gather | solution.py:244
  625.4 112.3 %all-gather.53.cloned.1.call-start = ((), (), s32[]{:S(2)}) async-start(), calls=%async_computation.21 | async-start | bytes 1310720 | tf_op jit(solution)/shard_map/all_gather | solution.py:352
  639.7 127.1 %all-gather.81.cloned.1.call-start = ((), (), s32[]{:S(2)}) async-start(), calls=%async_computation.45 | async-start | bytes 1310720 | tf_op jit(solution)/shard_map/all_gather | solution.py:353
  667.6 131.0 %reduce-scatter.20.cloned.1.call-start = ((), (), s32[]{:S(2)}) async-start(), calls=%async_computation.22 | async-start | bytes 1310720 | tf_op jit(solution)/shard_map/reduce_scatter | solution.py:381
  773.9 85.8 %all-gather.85.cloned.1.call-start = ((), (), s32[]{:S(2)}) async-start(), calls=%async_computation.47 | async-start | bytes 1310720 | tf_op jit(solution)/shard_map/all_gather | solution.py:313
  774.6 175.2 %all-reduce.12.cloned.1.call-start = ((), (), s32[]{:S(2)}) async-start(), calls=%async_computation.53 | async-start | bytes 4194304 | tf_op jit(solution)/shard_map/psum | solution.py:409
  840.0 137.9 %all-gather.55.cloned.1.call-start = ((), (), s32[]{:S(2)}) async-start(), calls=%async_computation.24 | async-start | bytes 1310720 | tf_op jit(solution)/shard_map/all_gather | solution.py:352
  876.3 131.2 %all-gather.57.cloned.1.call-start = ((), (), s32[]{:S(2)}) async-start(), calls=%async_computation.25 | async-start | bytes 1310720 | tf_op jit(solution)/shard_map/all_gather | solution.py:314
  960.7 75.4 %all-gather.87.cloned.1.call-start = ((), (), s32[]{:S(2)}) async-start(), calls=%async_computation.48 | async-start | bytes 1310720 | tf_op jit(solution)/shard_map/all_gather | solution.py:353
  962.7 105.3 %reduce-scatter.24.cloned.1.call-start = ((), (), s32[]{:S(2)}) async-start(), calls=%async_computation.26 | async-start | bytes 1310720 | tf_op jit(solution)/shard_map/reduce_scatter | solution.py:381
  1043.2 85.6 %all-gather.89.cloned.1.call-start = ((), (), s32[]{:S(2)}) async-start(), calls=%async_computation.49 | async-start | bytes 1310720 | tf_op jit(solution)/shard_map/all_gather | solution.py:313
  1043.9 174.5 %all-reduce.10.cloned.1.call-start = ((), (), s32[]{:S(2)}) async-start(), calls=%async_computation.52 | async-start | bytes 4194304 | tf_op jit(solution)/shard_map/psum | solution.py:409
  1109.1 137.4 %all-gather.59.cloned.1.call-start = ((), (), s32[]{:S(2)}) async-start(), calls=%async_computation.28 | async-start | bytes 1310720 | tf_op jit(solution)/shard_map/all_gather | solution.py:352
  1145.4 130.6 %all-gather.61.cloned.1.call-start = ((), (), s32[]{:S(2)}) async-start(), calls=%async_computation.29 | async-start | bytes 1310720 | tf_op jit(solution)/shard_map/all_gather | solution.py:314
  1228.4 76.0 %all-gather.91.cloned.1.call-start = ((), (), s32[]{:S(2)}) async-start(), calls=%async_computation.50 | async-start | bytes 1310720 | tf_op jit(solution)/shard_map/all_gather | solution.py:353
  1230.5 143.0 %reduce-scatter.28.cloned.1.call-start = ((), (), s32[]{:S(2)}) async-start(), calls=%async_computation.30 | async-start | bytes 1310720 | tf_op jit(solution)/shard_map/reduce_scatter | solution.py:381
  1309.4 68.6 %reduce-scatter.30.cloned.1.call-start = ((), (), s32[]{:S(2)}) async-start(), calls=%async_computation.31 | async-start | bytes 1310720 | tf_op jit(solution)/shard_map/reduce_scatter | solution.py:387
  1312.6 189.9 %reduce-scatter.18.cloned.1.call-start = ((), (), s32[]{:S(2)}) async-start(), calls=%async_computation.20 | async-start | bytes 1310720 | tf_op jit(solution)/shard_map/reduce_scatter | solution.py:274
  1332.8 173.6 %reduce-scatter.34.cloned.1.call-start = ((), (), s32[]{:S(2)}) async-start(), calls=%async_computation.33 | async-start | bytes 2621440 | tf_op jit(solution)/shard_map/reduce_scatter | solution.py:465
  1351.4 173.7 %all-reduce.8.cloned.1.call-start = ((), (), s32[]{:S(2)}) async-start(), calls=%async_computation.51 | async-start | bytes 4194304 | tf_op jit(solution)/shard_map/psum | solution.py:408
  1388.4 209.6 %reduce-scatter.32.cloned.1.call-start = ((), (), s32[]{:S(2)}) async-start(), calls=%async_computation.32 | async-start | bytes 7864320 | tf_op jit(solution)/shard_map/reduce_scatter | solution.py:456
  1425.0 262.8 %reduce-scatter.36.cloned.1.call-start = ((), (), s32[]{:S(2)}) async-start(), calls=%async_computation.34 | async-start | bytes 10485760 | tf_op jit(solution)/shard_map/reduce_scatter | solution.py:462
  1460.1 317.1 %reduce-scatter.38.cloned.1.call-start = ((), (), s32[]{:S(2)}) async-start(), calls=%async_computation.35 | async-start | bytes 10485760 | tf_op jit(solution)/shard_map/reduce_scatter | solution.py:468
  (191 other events, 3684.8 us)
Sparse Core Ops, SparseCore 0:
  10.2 30.7 all-gather.62
  43.4 69.4 all-gather.64
  124.3 26.6 all-gather.42
  181.4 87.4 all-gather.72
  270.6 87.6 all-gather.70
  360.1 35.1 all-gather.68
  399.4 27.1 reduce-scatter.13
  432.9 26.8 all-gather.44
  534.7 27.1 reduce-scatter.15
  567.5 26.7 all-gather.48
  596.4 27.4 all-gather.78
  625.2 27.4 all-gather.82
  711.0 26.6 all-gather.52
  740.1 26.6 all-gather.80
  770.9 27.7 reduce-scatter.19
  802.4 27.6 reduce-scatter.21
  831.7 27.9 all-gather.84
  863.2 86.5 all-reduce.11
  979.5 27.9 all-gather.56
  1040.2 27.7 reduce-scatter.23
  1071.4 27.7 reduce-scatter.25
  1100.9 27.9 all-gather.88
  1131.8 86.5 all-reduce.9
  1248.0 27.9 all-gather.60
  1309.6 27.7 reduce-scatter.27
  1340.5 27.7 reduce-scatter.29
  1370.9 27.1 reduce-scatter.17
  1401.8 33.8 reduce-scatter.33
  1438.0 87.0 all-reduce.7
  1528.2 69.7 reduce-scatter.31
  1601.4 86.3 reduce-scatter.35
  1690.9 86.3 reduce-scatter.37
  (9 shorter events, 234.6 us)
where the time goes:
time: 1800 us; the launch traced here: 1790 us
  waiting for transfers between devices  1150 us (64%)
  matrix products  338 us (19%)
  other arithmetic  113 us (6%)
  local copies, waits for them, and re-layouts  103 us (6%)
  blocking collectives  43.4 us (2%)
  starting transfers between devices  22.3 us (1%)
    psum x2, waiting for transfers between devices, shards(): lax.psum(grad_norm_two.astype(jnp.bfloat16), 'tensor').astype(jnp.float32)  145 us
    all_gather x1, waiting for transfers between devices, shards(): lax.all_gather(up_weight[0], 'ctx', axis=0, tiled=True)  89.3 us
    reduce_scatter x1, waiting for transfers between devices, shards(): lax.psum_scatter(grad_w_up.astype(jnp.bfloat16), 'ctx', scatter_dimension...  86.3 us
    all_gather x1, waiting for transfers between devices, shards(): lax.all_gather(down_weight[0], 'ctx', axis=1, tiled=True)  85.8 us
    reduce_scatter x1, waiting for transfers between devices, shards(): lax.psum_scatter(grad_w_down.astype(jnp.bfloat16), 'ctx', scatter_dimensi...  85.3 us
    all_gather x3, waiting for transfers between devices, shards(): value_all = lax.all_gather(backward_values_h, 'ctx', axis=0, tiled=True)  75.8 us
    all_gather x3, waiting for transfers between devices, shards(): lax.all_gather(forward_values_h, 'ctx', axis=0, tiled=True)  72.9 us
    all_gather x3, waiting for transfers between devices, shards(): grad_full = lax.all_gather(grad_out, 'tensor', axis=1, tiled=True)  65.1 us
  transfers between devices with their start and end apart: 45, of which 40 were waited for; matrix products, arithmetic and copies ran while one was open for 27% of the time, Pallas kernels for 0%

commit v1 on v0

--- a/solution.py
+++ b/solution.py
@@ -1,6 +1,11 @@
+import functools
+import math
+
 import jax
 import jax.numpy as jnp
 from jax import lax
+from jax.experimental import pallas as pl
+from jax.experimental.pallas import tpu as pltpu
 from jax.sharding import PartitionSpec as P
 
 ROT = 64
@@ -488,34 +493,1036 @@
     )
 
 
+AXES = ("section", "y", "x", "tensor")
+F32, BF16 = jnp.float32, jnp.bfloat16
+ROWS = 256
+WIDTH = 512
+MODEL = 2048
+HID = 1024
+A_ROWS = 3 * 256
+U_ROWS = 4 * 256
+O_ROWS = 2 * 128 + 2 * 512
+ANY = pl.BlockSpec(memory_space=pl.ANY)
+VMEM = pl.BlockSpec(memory_space=pltpu.VMEM)
+SMEM = pl.BlockSpec(memory_space=pltpu.SMEM)
+
+
+def across(value, axis, bits):
+    count = lax.axis_size(axis)
+    return lax.ppermute(value, axis, [(i, i ^ bits) for i in range(count)])
+
+
+def pick(value, index, axis=0):
+    return lax.dynamic_index_in_dim(value, index, axis, keepdims=False)
+
+
+def in_order(mine, theirs, bit, axis=0):
+    return jnp.where(
+        bit == 0, jnp.stack([mine, theirs], axis), jnp.stack([theirs, mine], axis)
+    )
+
+
+def routed(value, route):
+    pairs = []
+    for s in range(2):
+        for c in range(4):
+            for z in range(4):
+                ts, ty, tx, tz = route(s, c // 2, c % 2, z)
+                pairs.append(((s * 4 + c) * 4 + z, (ts * 4 + 2 * ty + tx) * 4 + tz))
+    return lax.ppermute(value, AXES, pairs)
+
+
+def dot_nn(a, b):
+    return lax.dot_general(a, b, (((1,), (0,)), ((), ())), preferred_element_type=F32)
+
+
+def dot_nt(a, b):
+    return lax.dot_general(a, b, (((1,), (1,)), ((), ())), preferred_element_type=F32)
+
+
+def dot_tn(a, b):
+    return lax.dot_general(a, b, (((0,), (0,)), ((), ())), preferred_element_type=F32)
+
+
+def call(body, name, ins, in_specs, outs, out_specs, scratch, limit=48):
+    return pl.pallas_call(
+        body,
+        out_shape=[jax.ShapeDtypeStruct(shape, dtype) for shape, dtype in outs],
+        in_specs=in_specs,
+        out_specs=out_specs,
+        scratch_shapes=scratch,
+        name=name,
+        cost_estimate=pl.CostEstimate(flops=1, bytes_accessed=1, transcendentals=0),
+        compiler_params=pltpu.CompilerParams(vmem_limit_bytes=limit * 2**20),
+    )(*ins)
+
+
+class Copies:
+    def __init__(self, sems):
+        self.sems = sems
+        self.count = 0
+
+    def start(self, source, target):
+        copy = pltpu.make_async_copy(source, target, self.sems.at[self.count])
+        self.count += 1
+        copy.start()
+        return copy
+
+
+def finish(copies):
+    for copy in copies:
+        copy.wait()
+
+
+def span(index, size):
+    return pl.ds(pl.multiple_of(index * size, size), size)
+
+
+def place_pieces(copies, pieces, target, idx):
+    x, z = idx[2], idx[3]
+    made = []
+    for n, piece in enumerate(pieces):
+        row = x if n < 4 else 1 - x
+        made.append(
+            copies.start(piece, target.at[span(row, ROWS), span(z ^ (n % 4), WIDTH)])
+        )
+    return made
+
+
+def piece_places(idx):
+    s, c = idx[0], 2 * idx[1] + idx[2]
+    return [(c ^ (n % 4), s ^ (n // 4)) for n in range(8)]
+
+
+def place_qkv(copies, pieces, base, target, idx):
+    made = []
+    for (c, k), piece in zip(piece_places(idx), pieces):
+        for t in range(3):
+            made.append(
+                copies.start(
+                    piece.at[pl.ds(base + t * 256, 256)],
+                    target.at[span(2 * c + k, 256), pl.ds(t * 256, 256)],
+                )
+            )
+    return made
+
+
+def place_up(copies, pieces, base, target, idx):
+    made = []
+    for u in range(4):
+        made.append([])
+        for (c, k), piece in zip(piece_places(idx), pieces):
+            made[-1].append(
+                copies.start(
+                    piece.at[pl.ds(base + u * 256, 256)],
+                    target.at[span(2 * c + k, 256), pl.ds(u * 256, 256)],
+                )
+            )
+    return made
+
+
+def place_inner(copies, pieces, base, target, idx):
+    made = []
+    for (c, k), piece in zip(piece_places(idx), pieces):
+        for half in range(2):
+            cols = span(2 * c + half, 256)
+            made.append(
+                copies.start(
+                    piece.at[pl.ds(base + half * 128, 128)], target.at[span(k, 128), cols]
+                )
+            )
+            made.append(
+                copies.start(
+                    piece.at[pl.ds(base + 256 + half * 512, 512)],
+                    target.at[pl.ds(pl.multiple_of(256 + k * 512, 256), 512), cols],
+                )
+            )
+    return made
+
+
+def prepare_a_body(idx, qkv, own, send):
+    s, x = idx[0], idx[2]
+    for k, to in ((1 - s, send), (s, own)):
+        for side, xx in ((0, x), (1, 1 - x)):
+            for t in range(3):
+                to[side, t * 256 : (t + 1) * 256, :] = qkv[t, span(k, 256), span(xx, 256)]
+
+
+def prepare_f_body(idx, out, up, down, u_own, u_send, o_own, o_send):
+    s, x = idx[0], idx[2]
+    for k, u_to, o_to in ((1 - s, u_send, o_send), (s, u_own, o_own)):
+        for side, xx in ((0, x), (1, 1 - x)):
+            for u in range(4):
+                u_to[side, u * 256 : (u + 1) * 256, :] = up[span(k, 256), span(xx * 4 + u, 256)]
+            for half in range(2):
+                cols = slice(half * 256, half * 256 + 256)
+                o_to[side, half * 128 : half * 128 + 128, :] = out[span(2 * xx + k, 128), cols]
+                o_to[side, 256 + half * 512 : 768 + half * 512, :] = down[
+                    span(2 * xx + k, 512), cols
+                ]
+
+
+def turn(block, tables, sign):
+    cosine, front, back = tables
+    return (
+        block * cosine
+        + sign * (pltpu.roll(block, 96, 1) * front + pltpu.roll(block, 32, 1) * back)
+    )
+
+
+def norm_body(base, idx, *refs):
+    pieces, weights = refs[:8], refs[8:16]
+    wide, bias, cosine, front, back = refs[16:21]
+    n_zero, n_one, xhat, q, kv, x_piece, inv_all = refs[21:28]
+    block_in, w, sems = refs[28:]
+    copies = Copies(sems)
+    loads = place_pieces(copies, pieces, block_in, idx)
+    fills = place_qkv(copies, weights, base, w, idx)
+    finish(loads)
+    step = 32
+
+    def rows_of(i, carry):
+        rows = pl.ds(pl.multiple_of(i * step, step), step)
+        values = block_in[rows, :].astype(F32)
+        centered = values - jnp.mean(values, axis=1, keepdims=True)
+        inv = lax.rsqrt(jnp.mean(centered * centered, axis=1, keepdims=True) + EPSILON)
+        normed = centered * inv
+        xhat[rows, :] = normed.astype(BF16)
+        n_zero[rows, :] = (normed * wide[0:1, :] + wide[2:3, :]).astype(BF16)
+        n_one[rows, :] = (normed * wide[1:2, :] + wide[3:4, :]).astype(BF16)
+        inv_all[rows, :] = jnp.broadcast_to(inv, (step, 128))
+        return carry
+
+    lax.fori_loop(0, 2 * ROWS // step, rows_of, 0)
+    finish(fills)
+    for half in range(2):
+        rows = pl.ds(half * ROWS, ROWS)
+        tables = (cosine[rows, :], front[rows, :], back[rows, :])
+        for t in range(3):
+            cols = pl.ds(t * 256, 256)
+            mixed = dot_nn(n_zero[rows, :], w[:, cols]) + bias[0:1, cols]
+            if t < 2:
+                turned = turn(mixed[:, :128], tables, 1.0).astype(BF16)
+                rest = mixed[:, 128:].astype(BF16)
+                if t == 0:
+                    q[rows, 0:128] = turned
+                    q[rows, 128:256] = rest
+                else:
+                    kv[rows, 0:128] = turned
+                    kv[rows, 128:256] = rest
+            else:
+                kv[rows, 256:512] = mixed.astype(BF16)
+    x_piece[...] = xhat[span(idx[2], ROWS), span(idx[3], WIDTH)]
+
+
+def up_body(base, idx, *refs):
+    weights = refs[:8]
+    n_one, bias, act, slope, w, sems = refs[8:]
+    fills = place_up(Copies(sems), weights, base, w, idx)
+    for u in range(4):
+        finish(fills[u])
+        cols = pl.ds(u * 256, 256)
+        for part in range(4):
+            rows = pl.ds(part * 128, 128)
+            value = dot_nn(n_one[rows, :], w[:, cols]) + bias[0:1, cols]
+            phi = 0.5 + 0.5 * lax.erf(value * (0.5**0.5))
+            act[rows, cols] = (value * phi).astype(BF16)
+            slope[rows, cols] = phi + value * (
+                jnp.exp(-0.5 * value * value) * (0.5 / math.pi) ** 0.5
+            )
+
+
+def attend_body(idx, lengths, q, kv_own, kv_other, prob, attn):
+    s, y = idx[0], idx[1]
+    step = 128
+    for part in range(2 * ROWS // step):
+        chunk = part * step // ROWS
+        rows = pl.ds(part * step, step)
+        first = (2 * chunk + s) * ROWS + part * step % ROWS
+        q_pos = first + lax.broadcasted_iota(jnp.int32, (step, 1), 0)
+        begin = jnp.zeros((step, 1), jnp.int32)
+        end = 0
+        for i in range(lengths.shape[1]):
+            end = end + lengths[y, i]
+            begin = jnp.where(q_pos >= end, end, begin)
+        scores = []
+        for side, kv in ((0, kv_own), (1, kv_other)):
+            column = lax.broadcasted_iota(jnp.int32, (1, 2 * ROWS), 1)
+            core = s if side == 0 else 1 - s
+            upper = (column >= ROWS).astype(jnp.int32)
+            k_pos = column + (upper + core) * ROWS
+            allowed = (k_pos <= q_pos) & (k_pos >= begin)
+            score = dot_nt(q[rows, :], kv[:, 0:256]) * (HD**-0.5)
+            scores.append(jnp.where(allowed, score, -1e30))
+        peak = jnp.maximum(
+            jnp.max(scores[0], axis=1, keepdims=True), jnp.max(scores[1], axis=1, keepdims=True)
+        )
+        masses = [jnp.exp(score - peak) for score in scores]
+        total = jnp.sum(masses[0], axis=1, keepdims=True) + jnp.sum(
+            masses[1], axis=1, keepdims=True
+        )
+        attended = 0.0
+        for side, kv in ((0, kv_own), (1, kv_other)):
+            share = masses[side] / total
+            prob[rows, pl.ds(side * 512, 512)] = share
+            attended = attended + dot_nn(share.astype(BF16), kv[:, 256:512])
+        attn[rows, :] = attended.astype(BF16)
+
+
+ORDER = (2, 3, 1, 0)
+
+
+def out_body(base, idx, *refs):
+    weights = refs[:8]
+    attn, act = refs[8:10]
+    sends, keeps = refs[10:14], refs[14:18]
+    w, sems = refs[18:]
+    fills = place_inner(Copies(sems), weights, base, w, idx)
+    x, z = idx[2], idx[3]
+    finish(fills)
+    for side, to in ((1, sends), (0, keeps)):
+        rows = span(x if side == 0 else 1 - x, ROWS)
+        for i, d in enumerate(ORDER):
+            cols = span(z ^ d, WIDTH)
+            value = dot_nn(attn[rows, :], w[0:256, cols]) + dot_nn(act[rows, :], w[256:1280, cols])
+            to[i][...] = value.astype(to[i].dtype)
+
+
+def add_body(kept, got, result):
+    result[...] = (kept[...] + got[...].astype(F32)).astype(BF16)
+
+
+def inner_grad(grad, weights, base, slope, outs, w, copies, idx, fills):
+    g_attn, d_up, grad_sum, up_sum = outs
+    grad_sum[...] = jnp.sum(grad[...].astype(F32), axis=0, keepdims=True)
+    finish(fills)
+    g_attn[...] = dot_nt(grad[...], w[0:256, :]).astype(BF16)
+    for u in range(4):
+        cols = pl.ds(u * 256, 256)
+        value = (
+            dot_nt(grad[...], w[pl.ds(256 + u * 256, 256), :]) * slope[:, cols]
+        ).astype(BF16)
+        d_up[:, cols] = value
+        up_sum[0:1, cols] = jnp.sum(value.astype(F32), axis=0, keepdims=True)
+
+
+def last_grad_body(base, idx, *refs):
+    pieces, weights, slope = refs[:8], refs[8:16], refs[16]
+    grad, outs = refs[17], refs[18:22]
+    w, sems = refs[22:]
+    copies = Copies(sems)
+    loads = place_pieces(copies, pieces, grad, idx)
+    fills = place_inner(copies, weights, base, w, idx)
+    finish(loads)
+    inner_grad(grad, weights, base, slope, outs, w, copies, idx, fills)
+
+
+def next_grad_body(base, idx, *refs):
+    pieces, weights, slope, later, xhat, inv_all = refs[:8], refs[8:16], *refs[16:20]
+    grad, grad_piece, outs = refs[20], refs[21], refs[22:26]
+    total, w, sems = refs[26:]
+    copies = Copies(sems)
+    loads = place_pieces(copies, pieces, total, idx)
+    fills = place_inner(copies, weights, base, w, idx)
+    finish(loads)
+    step = 32
+
+    def rows_of(i, carry):
+        rows = pl.ds(pl.multiple_of(i * step, step), step)
+        value = total[rows, :].astype(F32)
+        normed = xhat[rows, :].astype(F32)
+        mean = jnp.mean(value, axis=1, keepdims=True)
+        slant = jnp.mean(value * normed, axis=1, keepdims=True)
+        value = inv_all[rows, 0:1] * (value - mean - normed * slant)
+        grad[rows, :] = (later[rows, :].astype(F32) + value).astype(BF16)
+        return carry
+
+    lax.fori_loop(0, 2 * ROWS // step, rows_of, 0)
+    grad_piece[...] = grad[span(idx[2], ROWS), span(idx[3], WIDTH)]
+    inner_grad(grad, weights, base, slope, outs, w, copies, idx, fills)
+
+
+def attend_back_body(q, kv_own, kv_other, prob, g_attn, d_q, keep, send, d_score, share):
+    scaling = HD**-0.5
+    step = 128
+    for part in range(2 * ROWS // step):
+        rows = pl.ds(part * step, step)
+        weights = prob[rows, :]
+        d_prob = [dot_nt(g_attn[rows, :], kv[:, 256:512]) for kv in (kv_own, kv_other)]
+        halves = [weights[:, :512], weights[:, 512:]]
+        delta = jnp.sum(halves[0] * d_prob[0], axis=1, keepdims=True) + jnp.sum(
+            halves[1] * d_prob[1], axis=1, keepdims=True
+        )
+        total = 0.0
+        for side, kv in ((0, kv_own), (1, kv_other)):
+            value = (halves[side] * (d_prob[side] - delta)).astype(BF16)
+            d_score[rows, pl.ds(side * 512, 512)] = value
+            total = total + dot_nn(value, kv[:, 0:256])
+        d_q[rows, :] = total * scaling
+        share[rows, :] = weights.astype(BF16)
+    keep[:, 0:256] = dot_tn(d_score[:, 0:512], q[...]) * scaling
+    keep[:, 256:512] = dot_tn(share[:, 0:512], g_attn[...])
+    send[:, 0:256] = (dot_tn(d_score[:, 512:1024], q[...]) * scaling).astype(BF16)
+    send[:, 256:512] = dot_tn(share[:, 512:1024], g_attn[...]).astype(BF16)
+
+
+def outer_u_body(idx, n_one, d_up, keep, send):
+    s, c = idx[0], pl.program_id(0)
+    for k, to in ((1 - s, send), (s, keep)):
+        value = dot_tn(n_one[:, span(2 * c + k, 256)], d_up[...]).astype(BF16)
+        for u in range(4):
+            to[0, u * 256 : (u + 1) * 256, :] = value[:, u * 256 : (u + 1) * 256]
+
+
+def outer_o_body(idx, attn, act, grad, keep, send):
+    s, c = idx[0], pl.program_id(0)
+    g_cols = grad[:, span(c, WIDTH)]
+    for k, to in ((1 - s, send), (s, keep)):
+        value = dot_tn(attn[:, span(k, 128)], g_cols).astype(BF16)
+        to[0, 0:128, :] = value[:, :256]
+        to[0, 128:256, :] = value[:, 256:]
+        value = dot_tn(act[:, span(k, 512)], g_cols).astype(BF16)
+        to[0, 256:768, :] = value[:, :256]
+        to[0, 768:1280, :] = value[:, 256:]
+
+
+def outer_a_body(idx, n_zero, d_mix, keep, send):
+    s, c = idx[0], pl.program_id(0)
+    for k, to in ((1 - s, send), (s, keep)):
+        value = dot_tn(n_zero[:, span(2 * c + k, 256)], d_mix[...]).astype(BF16)
+        for t in range(3):
+            to[0, t * 256 : (t + 1) * 256, :] = value[:, t * 256 : (t + 1) * 256]
+
+
+class Part:
+    def __init__(self, ref, k, base):
+        self.ref, self.k, self.base = ref, k, base
+
+    def __setitem__(self, at, value):
+        rows = pl.ds(self.base + at[1].start, at[1].stop - at[1].start)
+        self.ref[self.k, 0, 0, rows, :] = value
+
+
+def outer_uo_body(idx, n_one, d_up, attn, act, grad, result, base=0):
+    s = idx[0]
+    outer_u_body(idx, n_one, d_up, Part(result, s, base), Part(result, 1 - s, base))
+    base = base + U_ROWS
+    outer_o_body(idx, attn, act, grad, Part(result, s, base), Part(result, 1 - s, base))
+
+
+def outer_all_body(idx, n_zero, d_mix, *refs):
+    s, result = idx[0], refs[5]
+    outer_a_body(idx, n_zero, d_mix, Part(result, s, 0), Part(result, 1 - s, 0))
+    outer_uo_body(idx, *refs, base=A_ROWS)
+
+
+def outer(body, name, idx, ins, rows):
+    if rows == A_ROWS:
+        outs = [jax.ShapeDtypeStruct((4, rows, 256), BF16)] * 2
+        specs = [pl.BlockSpec((1, rows, 256), lambda c: (c, 0, 0))] * 2
+    else:
+        outs = jax.ShapeDtypeStruct((2, 2, 2, rows, 256), BF16)
+        specs = pl.BlockSpec((2, 1, 1, rows, 256), lambda c: (0, c // 2, c % 2, 0, 0))
+    return pl.pallas_call(
+        body,
+        grid=(4,),
+        out_shape=outs,
+        in_specs=[SMEM] + [pl.BlockSpec(v.shape, lambda c: (0, 0)) for v in ins],
+        out_specs=specs,
+        name=name,
+        cost_estimate=pl.CostEstimate(flops=1, bytes_accessed=1, transcendentals=0),
+        compiler_params=pltpu.CompilerParams(vmem_limit_bytes=48 * 2**20),
+    )(idx, *ins)
+
+
+def mix_grad_body(base_a, base_u, idx, *refs):
+    a_weights, u_weights = refs[:8], refs[8:16]
+    d_q, d_kv, d_kv_got, cosine, front, back, d_up, xhat, wide = refs[16:25]
+    d_mix, mix_sum, norm_sum, stats = refs[25:29]
+    sends, keeps = refs[29:33], refs[33:37]
+    w_a, w_u, sums, sems = refs[37:]
+    copies = Copies(sems)
+    fills = place_qkv(copies, a_weights, base_a, w_a, idx)
+    for group in place_up(copies, u_weights, base_u, w_u, idx):
+        fills += group
+    x, z = idx[2], idx[3]
+    for half in range(2):
+        rows = pl.ds(half * ROWS, ROWS)
+        tables = (cosine[rows, :], front[rows, :], back[rows, :])
+        got = d_kv_got[rows, :].astype(F32)
+        total = d_kv[rows, :] + got
+        d_mix[rows, 0:128] = turn(d_q[rows, 0:128], tables, -1.0).astype(BF16)
+        d_mix[rows, 128:256] = d_q[rows, 128:256].astype(BF16)
+        d_mix[rows, 256:384] = turn(total[:, 0:128], tables, -1.0).astype(BF16)
+        d_mix[rows, 384:768] = total[:, 128:512].astype(BF16)
+    mix_sum[...] = jnp.sum(d_mix[...].astype(F32), axis=0, keepdims=True)
+    sums[...] = jnp.zeros_like(sums)
+    finish(fills)
+    for i, d in enumerate(ORDER):
+        cols = span(z ^ d, WIDTH)
+        columns = []
+        for side in (1, 0):
+            rows = span(x if side == 0 else 1 - x, ROWS)
+            dn_zero = dot_nt(d_mix[rows, :], w_a[cols, :])
+            dn_one = dot_nt(d_up[rows, :], w_u[cols, :])
+            normed = xhat[rows, cols].astype(F32)
+            mixed = dn_zero * wide[0:1, cols] + dn_one * wide[1:2, cols]
+            sums[rows, 0:1] += jnp.sum(mixed, axis=1, keepdims=True)
+            sums[rows, 1:2] += jnp.sum(mixed * normed, axis=1, keepdims=True)
+            columns.append(
+                [
+                    jnp.sum(value, axis=0, keepdims=True)
+                    for value in (dn_zero * normed, dn_one * normed, dn_zero, dn_one)
+                ]
+            )
+            if side == 1:
+                sends[i][...] = mixed.astype(BF16)
+            else:
+                keeps[i][...] = mixed
+        for j in range(4):
+            norm_sum[j : j + 1, cols] = columns[0][j] + columns[1][j]
+    stats[...] = jnp.transpose(sums[...])[0:8, :]
+
+
+def input_grad_body(idx, kept, got, far_a, far_b, far_c, stats, xhat, inv, grad, result):
+    x = idx[2]
+    rows = stats[:, span(x, ROWS)] * (1.0 / MODEL)
+    columns = jnp.transpose(jnp.concatenate([rows] * 16, axis=0))
+    total = kept[...] + got[...].astype(F32)
+    total = total + far_a[...].astype(F32) + far_b[...].astype(F32) + far_c[...].astype(F32)
+    normed = xhat[...].astype(F32)
+    value = inv[span(x, ROWS), 0:1] * (total - columns[:, 0:1] - normed * columns[:, 1:2])
+    result[...] = (grad[...].astype(F32) + value).astype(BF16)
+
+
+def small_sums_body(idx, *refs):
+    result = refs[8]
+    x, z = idx[2], idx[3]
+    result[...] = jnp.zeros_like(result)
+    for l in range(2):
+        norm, mix, up, grad = refs[4 * l : 4 * l + 4]
+        first = 12 * l
+        result[first : first + 4, :] = norm[:, span(z, WIDTH)]
+        for d in (1, 2, 3):
+            base = 16 + 8 * d + 4 * l
+            result[base : base + 4, :] = norm[:, span(z ^ d, WIDTH)]
+        for t in range(3):
+            result[first + 4 + t : first + 5 + t, span(x, 256)] = mix[0:1, t * 256 : (t + 1) * 256]
+        for half in range(2):
+            result[pl.ds(first + 7 + 2 * x + half, 1), :] = up[0:1, half * 512 : (half + 1) * 512]
+        result[first + 11 : first + 12, :] = jnp.where(x == 0, grad[0:1, span(z, WIDTH)], 0.0)
+
+
+def unpack_a_body(idx, own, got, qkv):
+    s, x = idx[0], idx[2]
+    for k, pair in ((s, own), (1 - s, got)):
+        for side, xx in ((0, x), (1, 1 - x)):
+            for t in range(3):
+                qkv[t, span(k, 256), span(xx, 256)] = pair[side, t * 256 : (t + 1) * 256, :].astype(F32)
+
+
+def unpack_uo_body(idx, own, got, up, out, down):
+    s, x = idx[0], idx[2]
+    for k, pair in ((s, own), (1 - s, got)):
+        for side, xx in ((0, x), (1, 1 - x)):
+            for u in range(4):
+                up[span(k, 256), span(xx * 4 + u, 256)] = pair[
+                    side, u * 256 : (u + 1) * 256, :
+                ].astype(F32)
+            for half in range(2):
+                cols = slice(half * 256, half * 256 + 256)
+                first = U_ROWS + half * 128
+                out[span(2 * xx + k, 128), cols] = pair[side, first : first + 128, :].astype(F32)
+                first = U_ROWS + 256 + half * 512
+                down[span(2 * xx + k, 512), cols] = pair[side, first : first + 512, :].astype(F32)
+
+
+def after(value, *done):
+    return lax.optimization_barrier((value, *done))[0]
+
+
+def relay_shards(
+    block_input,
+    out_cotangent,
+    doc_lengths,
+    norm_gain,
+    norm_bias,
+    qkv_weight,
+    qkv_bias,
+    out_weight,
+    out_bias,
+    up_weight,
+    up_bias,
+    down_weight,
+    down_bias,
+):
+    s = lax.axis_index("section")
+    y = lax.axis_index("y")
+    x = lax.axis_index("x")
+    z = lax.axis_index("tensor")
+    idx = jnp.stack([s, y, x, z]).astype(jnp.int32)
+    dma = pltpu.SemaphoreType.DMA
+
+    def spread_near(piece):
+        near = [piece] + [None] * 3
+        for d in (2, 3, 1):
+            near[d] = across(piece, "tensor", d)
+        return near
+
+    def spread_far(near, *done):
+        far = [None] * 4
+        for d in (0, 2, 3, 1):
+            far[d] = across(after(near[d], *done) if done else near[d], "x", 1)
+        return near + far
+
+    def spread(piece):
+        return spread_far(spread_near(piece))
+
+    def sum_over_x(sends):
+        return [across(send, "x", 1) for send in sends]
+
+    def added(keeps, got, i, *done):
+        part = after(got[i], *done) if done else got[i]
+        return call(
+            add_body,
+            "add_piece",
+            (keeps[i], part),
+            [VMEM] * 2,
+            [((ROWS, WIDTH), BF16)],
+            [VMEM],
+            [],
+        )[0]
+
+    def sum_over_tensor(keeps, got, between=None, *done):
+        totals = [added(keeps, got, i, *done) for i in range(2)]
+        extra = None
+        if between is not None:
+            extra = between(totals)
+        last = added(keeps, got, 2, *done, *([] if extra is None else jax.tree.leaves(extra)))
+        far = [across(v, "tensor", d) for v, d in zip(totals + [last], ORDER)]
+        return (far, extra) if between is not None else far
+
+    def summed(keeps, got, far):
+        total = keeps[3] + got[3].astype(F32)
+        return total + far[0].astype(F32) + far[1].astype(F32) + far[2].astype(F32)
+
+    to_piece = lambda ss, yy, xx, zz: (xx, ss, yy, zz)
+    input_piece = routed(pick(block_input, s), to_piece)
+    first = spread(input_piece)
+
+    a_own, a_send = call(
+        prepare_a_body,
+        "prepare_a",
+        (idx, qkv_weight[0].transpose(1, 0, 2)),
+        [SMEM, VMEM],
+        [((2, A_ROWS, 256), BF16)] * 2,
+        [VMEM] * 2,
+        [],
+    )
+    a_got = across(a_send, "section", 1)
+    u_own, u_send, o_own, o_send = call(
+        prepare_f_body,
+        "prepare_f",
+        (idx, out_weight[0], up_weight[0], down_weight[0]),
+        [SMEM] + [VMEM] * 3,
+        [((2, U_ROWS, 256), BF16)] * 2 + [((2, O_ROWS, 256), BF16)] * 2,
+        [VMEM] * 4,
+        [],
+    )
+    u_got = across(u_send, "section", 1)
+    o_got = across(o_send, "section", 1)
+    x_chain, y_chain = [], []
+
+    def fetch(own, got, layer, x_done=(), m_done=(), r_done=(), k_done=()):
+        mine, other = [jnp.where(s == layer, own[i], got[i]) for i in range(2)]
+        other = after(other, *x_chain[-1:], *x_done)
+        pieces = [mine, across(other, "x", 1)]
+        x_chain.append(pieces[1])
+        for value, done in ((mine, m_done), (pieces[1], r_done)):
+            pieces.append(across(after(value, *y_chain[-2:-1], *done), "y", 1))
+            y_chain.append(pieces[-1])
+        bound = [after(v, *k_done) for v in pieces] if k_done else pieces
+        return pieces + [across(v, "section", 1) for v in bound]
+
+    small = jnp.concatenate(
+        [norm_gain[0], norm_bias[0], out_bias, down_bias, qkv_bias[0], up_bias[0].reshape(4, WIDTH)],
+        axis=0,
+    )
+    small = in_order(small, across(small, "section", 1), s)
+    norms = small[:, :4].reshape(8, WIDTH)
+    pair = in_order(norms, across(norms, "tensor", 2), z // 2)
+    near = across(pair, "tensor", 1)
+    quads = in_order(pair, near, z % 2, 1)
+    wide = quads.transpose(2, 0, 1, 3).reshape(2, 4, MODEL).astype(F32)
+    bias_qkv = pick(small[:, 6:9].reshape(2, 3, 2, HD), x, 2).reshape(2, 1, 3 * HD).astype(F32)
+    bias_up = pick(small[:, 9:].reshape(2, 2, HID), x, 1).reshape(2, 1, HID).astype(F32)
+    bias_piece = small[:, 4:5].astype(F32) + small[:, 5:6].astype(F32)
+
+    rows = jnp.arange(ROWS, dtype=jnp.int32)
+    own_pos = jnp.concatenate([(2 * i + s) * ROWS + rows for i in range(2)])
+    _, doc_pos = doc_layout(pick(doc_lengths, y), own_pos)
+    cosine, sine = rotary_tables(doc_pos, ROT)
+    cosine, sine = cosine[:, 0], sine[:, 0]
+    blank = jnp.zeros((2 * ROWS, 32), F32)
+    ones = jnp.ones((2 * ROWS, 64), F32)
+    tables = (
+        jnp.concatenate([cosine, cosine, ones], axis=1),
+        jnp.concatenate([-sine, blank, blank, blank], axis=1),
+        jnp.concatenate([blank, sine, blank, blank], axis=1),
+    )
+    full = (2 * ROWS, MODEL)
+
+    wa_zero = fetch(a_own, a_got, 0)
+    wu_zero = fetch(u_own, u_got, 0, (first[5],))
+
+    def norm(layer, pieces, w_a, base):
+        return call(
+            functools.partial(norm_body, base),
+            "norm_qkv",
+            (idx, *pieces, *w_a, wide[layer], bias_qkv[layer], *tables),
+            [SMEM] + [ANY] * 16 + [VMEM] * 5,
+            [
+                (full, BF16),
+                (full, BF16),
+                (full, BF16),
+                ((512, 256), BF16),
+                ((512, 512), BF16),
+                ((ROWS, WIDTH), BF16),
+                ((512, 128), F32),
+            ],
+            [VMEM] * 7,
+            [
+                pltpu.VMEM(full, BF16),
+                pltpu.VMEM((MODEL, 768), BF16),
+                dma((32,)),
+            ],
+        )
+
+    def upward(layer, n_one, w_u, base):
+        return call(
+            functools.partial(up_body, base),
+            "up_gelu",
+            (idx, *w_u, n_one, bias_up[layer]),
+            [SMEM] + [ANY] * 8 + [VMEM] * 2,
+            [((512, HID), BF16), ((512, HID), F32)],
+            [VMEM] * 2,
+            [pltpu.VMEM((MODEL, HID), BF16), dma((32,))],
+        )
+
+    def attend(q, kv, kv_other):
+        return call(
+            attend_body,
+            "attend",
+            (idx, doc_lengths, q, kv, kv_other),
+            [SMEM] * 2 + [VMEM] * 3,
+            [((512, 1024), F32), ((512, 256), BF16)],
+            [VMEM] * 2,
+            [],
+        )
+
+    def downward(attn, act, w_o, base):
+        parts = call(
+            functools.partial(out_body, base),
+            "out_down",
+            (idx, *w_o, attn, act),
+            [SMEM] + [ANY] * 8 + [VMEM] * 2,
+            [((ROWS, WIDTH), BF16)] * 4 + [((ROWS, WIDTH), F32)] * 4,
+            [VMEM] * 8,
+            [pltpu.VMEM((1280, MODEL), BF16), dma((32,))],
+        )
+        return parts[:4], parts[4:]
+
+    def state_of(layer, piece, total):
+        return (piece.astype(F32) + total + bias_piece[layer]).astype(BF16)
+
+    inner_outs = [
+        ((512, 256), BF16),
+        ((512, HID), BF16),
+        ((1, MODEL), F32),
+        ((1, HID), F32),
+    ]
+
+    def attend_back(q, kv, kv_other, prob, g_attn):
+        return call(
+            attend_back_body,
+            "attend_back",
+            (q, kv, kv_other, prob, g_attn),
+            [VMEM] * 5,
+            [((512, 256), F32), ((512, 512), F32), ((512, 512), BF16)],
+            [VMEM] * 3,
+            [pltpu.VMEM((512, 1024), BF16), pltpu.VMEM((512, 1024), BF16)],
+        )
+
+    def mix_grad(layer, d_q, d_kv, d_kv_got, d_up, xhat, w_a, w_u, bases):
+        outs = call(
+            functools.partial(mix_grad_body, *bases),
+            "grad_mix",
+            (idx, *w_a, *w_u, d_q, d_kv, d_kv_got, *tables, d_up, xhat, wide[layer]),
+            [SMEM] + [ANY] * 16 + [VMEM] * 9,
+            [((512, 768), BF16), ((1, 768), F32), ((4, MODEL), F32), ((8, 512), F32)]
+            + [((ROWS, WIDTH), BF16)] * 4
+            + [((ROWS, WIDTH), F32)] * 4,
+            [VMEM] * 12,
+            [
+                pltpu.VMEM((MODEL, 768), BF16),
+                pltpu.VMEM((MODEL, HID), BF16),
+                pltpu.VMEM((512, 128), F32),
+                dma((64,)),
+            ],
+        )
+        return outs[:4], outs[4:8], outs[8:]
+
+    def over_cores(pair):
+        keep, send = pair
+        got = across(send, "section", 1)
+        shape = (2, 2) + keep.shape[1:]
+        return keep.reshape(shape), got.reshape(shape)
+
+    def summed_rows(grad):
+        total = lax.psum_scatter(
+            grad.reshape((4,) + grad.shape[2:]), ("section", "y"), scatter_dimension=0, tiled=True
+        )
+        return total[0], grad
+
+    def y_part(keep, got):
+        return (pick(keep, 1 - y).astype(F32) + pick(got, 1 - y).astype(F32)).astype(BF16)
+
+    def x_part(keep, got, y_got, xx):
+        at = lambda value: pick(pick(value, y), xx).astype(F32)
+        return (at(keep) + at(got) + pick(y_got, xx).astype(F32)).astype(BF16)
+
+    n_zero0, n_one0, xhat0, q0, kv0, x_piece0, inv0 = norm(0, first, wa_zero, 0)
+    kv_other0 = across(kv0, "section", 1)
+    cotangent_piece = routed(pick(out_cotangent, s), to_piece)
+    act0, slope0 = upward(0, n_one0, wu_zero, 0)
+    prob0, attn0 = attend(q0, kv0, kv_other0)
+    wo_zero = fetch(o_own, o_got, 0, (kv0,), (kv0,), (act0,))
+    wa_one = fetch(a_own, a_got, 1, (kv0,), (act0,), ())
+    sends, keeps = downward(attn0, act0, wo_zero, 0)
+    got = sum_over_x(sends)
+    wu_one = fetch(u_own, u_got, 1, (act0,), (sends[0],), (got[0],))
+    far = sum_over_tensor(keeps, got)
+    state_zero = state_of(0, input_piece, summed(keeps, got, far))
+    wo_one = fetch(o_own, o_got, 1, (got[3],), (state_zero,), (state_zero,))
+    second = spread(state_zero)
+
+    n_zero1, n_one1, xhat1, q1, kv1, _, inv1 = norm(1, second, wa_one, 0)
+    kv_other1 = across(kv1, "section", 1)
+    last_grad = spread_far(spread_near(after(cotangent_piece, kv0)), n_one1)
+    act1, slope1 = upward(1, n_one1, wu_one, 0)
+    prob1, attn1 = attend(q1, kv1, kv_other1)
+    sends1, keeps1 = downward(attn1, act1, wo_one, 0)
+    state_got = sum_over_x(sends1)
+
+    grad1, g_attn1, d_up1, grad_sum1, up_sum1 = call(
+        functools.partial(last_grad_body, 0),
+        "last_grad",
+        (idx, *last_grad[:7], after(last_grad[7], sends1[0]), *wo_one, slope1),
+        [SMEM] + [ANY] * 16 + [VMEM],
+        [(full, BF16)] + inner_outs,
+        [VMEM] * 5,
+        [pltpu.VMEM((1280, MODEL), BF16), dma((40,))],
+    )
+    d_q, d_kv, d_kv_send = attend_back(q1, kv1, kv_other1, prob1, g_attn1)
+    d_kv_got = across(d_kv_send, "section", 1)
+    uo_grad = outer(
+        outer_uo_body,
+        "outer_uo",
+        idx,
+        (n_one1, after(d_up1, d_q), attn1, act1, grad1),
+        U_ROWS + O_ROWS,
+    )
+    (d_mix1, mix_sum1, norm_sum1, _), sends, keeps = mix_grad(
+        1,
+        after(d_q, uo_grad, *state_got),
+        d_kv,
+        d_kv_got,
+        d_up1,
+        xhat1,
+        wa_one,
+        wu_one,
+        (0, 0),
+    )
+    uo_one, _ = summed_rows(after(uo_grad, norm_sum1))
+    got = sum_over_x(sends)
+    far = sum_over_tensor(keeps, got)
+    mixed_piece = summed(keeps, got, far).astype(BF16)
+    mixed = spread(mixed_piece)
+
+    grad0, grad_one_piece, g_attn0, d_up0, grad_sum0, up_sum0 = call(
+        functools.partial(next_grad_body, 0),
+        "next_grad",
+        (idx, *mixed, *wo_zero, slope0, grad1, xhat1, inv1),
+        [SMEM] + [ANY] * 16 + [VMEM] * 4,
+        [(full, BF16), ((ROWS, WIDTH), BF16)] + inner_outs,
+        [VMEM] * 6,
+        [pltpu.VMEM(full, BF16), pltpu.VMEM((1280, MODEL), BF16), dma((40,))],
+    )
+    both_grad = outer(
+        outer_all_body,
+        "outer_all",
+        idx,
+        (n_zero1, d_mix1, n_one0, d_up0, attn0, act0, grad0),
+        A_ROWS + U_ROWS + O_ROWS,
+    )
+    both_sum, _ = summed_rows(after(both_grad, uo_one))
+    d_q, d_kv, d_kv_send = attend_back(q0, kv0, kv_other0, prob0, after(g_attn0, both_grad))
+    d_kv_got = across(d_kv_send, "section", 1)
+    (d_mix0, mix_sum0, norm_sum0, stats), sends, keeps = mix_grad(
+        0,
+        d_q,
+        d_kv,
+        d_kv_got,
+        d_up0,
+        xhat0,
+        wa_zero,
+        wu_zero,
+        (0, 0),
+    )
+    got = sum_over_x(sends)
+    (sums,) = call(
+        small_sums_body,
+        "small_sums",
+        (
+            idx,
+            norm_sum0,
+            mix_sum0,
+            up_sum0,
+            grad_sum0,
+            norm_sum1,
+            mix_sum1,
+            up_sum1,
+            grad_sum1,
+        ),
+        [SMEM] + [VMEM] * 8,
+        [((48, WIDTH), F32)],
+        [VMEM],
+        [],
+    )
+    sums_far = [across(sums[16 + 8 * d : 24 + 8 * d], "tensor", d) for d in (1, 2, 3)]
+    for bits in (1, 2):
+        stats = stats + across(stats, "tensor", bits)
+    sums_far = (sums_far[0] + sums_far[1] + sums_far[2]).reshape(2, 4, WIDTH)
+    sums = sums[:24].reshape(2, 12, WIDTH) + jnp.pad(sums_far, ((0, 0), (0, 8), (0, 0)))
+    sums = jnp.concatenate([sums.reshape(24, WIDTH), stats], axis=0)
+    totals = [added(keeps, got, i) for i in range(3)]
+    far = [across(v, "tensor", d) for v, d in zip(totals, ORDER)]
+    uo_one = after(uo_one, *got)
+    uo_send = pick(uo_one, 1 - x)
+    uo_x = across(uo_send, "x", 1)
+    uo_one = (pick(uo_one, x), uo_x)
+    a_grad = outer(outer_a_body, "outer_a", idx, (after(n_zero0, uo_x, *far), d_mix0), A_ROWS)
+    a_sum = over_cores(a_grad)
+    sums = sums + across(after(sums, *totals), "x", 1)
+    sums, stats = sums[:24].reshape(2, 12, WIDTH), sums[24:]
+    a_part = y_part(a_sum[0], after(a_sum[1], stats))
+    sums_y = across(after(sums, a_part), "y", 1)
+    a_y = across(a_part, "y", 1)
+    state_far = sum_over_tensor(keeps1, state_got, None, uo_send)
+    (grad_zero_piece,) = call(
+        input_grad_body,
+        "input_grad",
+        (idx, keeps[3], got[3], *far, stats, x_piece0, inv0, grad_one_piece),
+        [SMEM] + [VMEM] * 9,
+        [((ROWS, WIDTH), BF16)],
+        [VMEM],
+        [],
+    )
+    both_sum = after(both_sum, uo_x, grad_zero_piece, a_part)
+    both = (pick(both_sum, x), across(pick(both_sum, 1 - x), "x", 1))
+    sums = sums + sums_y
+    sums = pick(sums, s) + across(pick(sums, 1 - s), "section", 1)
+    state_far[2] = after(state_far[2], a_y, sums_y)
+    state_one = state_of(1, state_zero, summed(keeps1, state_got, state_far))
+    a_zero = (x_part(*a_sum, a_y, x), across(x_part(*a_sum, a_y, 1 - x), "x", 1))
+
+    for_zero = jnp.stack([state_zero, grad_zero_piece])
+    for_one = jnp.stack([state_one, grad_one_piece])
+    to_same = routed(
+        jnp.where(y == 0, for_zero, for_one), lambda ss, yy, xx, zz: (yy, xx, ss, zz)
+    )
+    to_other = routed(
+        jnp.where(y == 0, for_one, for_zero), lambda ss, yy, xx, zz: (1 - yy, xx, ss, zz)
+    )
+    placed = in_order(to_same, to_other, s, 1)
+
+    both = after(both, placed)
+
+    def unpacked(body, name, zero, one, shapes):
+        zero, one = jnp.stack(zero), jnp.stack(one)
+        own = jnp.where(s == 0, zero, one)
+        got = across(jnp.where(s == 0, one, zero), "section", 1)
+        return call(
+            body,
+            name,
+            (idx, own, got),
+            [SMEM] + [VMEM] * 2,
+            [(shape, F32) for shape in shapes],
+            [VMEM] * len(shapes),
+            [],
+        )
+
+    out_up, out_out, out_down = unpacked(
+        unpack_uo_body,
+        "unpack_uo",
+        [v[A_ROWS:] for v in both],
+        uo_one,
+        [(WIDTH, 2 * HID), (WIDTH, WIDTH), (2 * HID, WIDTH)],
+    )
+    (out_qkv,) = unpacked(
+        unpack_a_body, "unpack_a", a_zero, [v[:A_ROWS] for v in both], [(3, WIDTH, WIDTH)]
+    )
+    return (
+        placed[0][None],
+        placed[1][None],
+        sums[None, 0:2],
+        sums[None, 2:4],
+        out_qkv.transpose(1, 0, 2)[None],
+        sums[None, 4:7],
+        out_out[None],
+        sums[11:12],
+        out_up[None],
+        sums[7:11].reshape(1, 2 * HID),
+        out_down[None],
+        sums[11:12],
+    )
+
+
 def solution(mesh):
+    sizes = dict(mesh.shape)
+    body, ctx = shards, "ctx"
+    if (sizes["section"], sizes["ctx"], sizes["tensor"]) == (2, 4, 4):
+        body = relay_shards
+        devices = mesh.devices.reshape(2, 2, 2, 4)
+        mesh = jax.sharding.Mesh(devices, ("section", "y", "x", "tensor"))
+        ctx = ("y", "x")
     in_specs = (
-        P(None, "ctx", "tensor"),
-        P(None, "ctx", "tensor"),
+        P(None, ctx, "tensor"),
+        P(None, ctx, "tensor"),
         P(),
         P("section", None, "tensor"),
         P("section", None, "tensor"),
-        P("section", "ctx", None, "tensor"),
+        P("section", ctx, None, "tensor"),
         P("section", None, "tensor"),
-        P("section", "tensor", "ctx"),
+        P("section", "tensor", ctx),
         P("section", "tensor"),
-        P("section", "ctx", "tensor"),
+        P("section", ctx, "tensor"),
         P("section", "tensor"),
-        P("section", "tensor", "ctx"),
+        P("section", "tensor", ctx),
         P("section", "tensor"),
     )
     out_specs = (
-        P("section", None, "ctx", "tensor"),
-        P("section", None, "ctx", "tensor"),
+        P("section", None, ctx, "tensor"),
+        P("section", None, ctx, "tensor"),
         P("section", None, "tensor"),
         P("section", None, "tensor"),
-        P("section", "ctx", None, "tensor"),
+        P("section", ctx, None, "tensor"),
         P("section", None, "tensor"),
-        P("section", "tensor", "ctx"),
+        P("section", "tensor", ctx),
         P("section", "tensor"),
-        P("section", "ctx", "tensor"),
+        P("section", ctx, "tensor"),
         P("section", "tensor"),
-        P("section", "tensor", "ctx"),
+        P("section", "tensor", ctx),
         P("section", "tensor"),
     )
-    return jax.shard_map(shards, mesh=mesh, in_specs=in_specs, out_specs=out_specs, check_vma=False)
+    return jax.shard_map(body, mesh=mesh, in_specs=in_specs, out_specs=out_specs, check_vma=False)

time: 1800 us -> 653 us (0.36)
  waiting for transfers between devices: 1150 us -> 242 us
  matrix products: 338 us -> 0 us
  Pallas kernels: 0 us -> 144 us
  starting transfers between devices: 22.3 us -> 148 us
  other arithmetic: 113 us -> 22.4 us
  blocking collectives: 43.4 us -> 0 us
  local copies, waits for them, and re-layouts: 103 us -> 72.3 us
    all_gather x25 -> x0, waiting for transfers between devices: 651 us -> none  [the longest x1 89.3 us: shards(): lax.all_gather(up_weight[0], 'ctx', axis=0, tiled=True)]
    dot_general x60 -> x0, matrix products: 338 us -> none  [the longest x3 46.7 us: shards(): jnp.dot(forward_activated, w_down, preferred_element_type=jnp.float32)]
    reduce_scatter x13 -> x2, waiting for transfers between devices: 329 us -> 0.01 us  [summed_rows(): lax.psum_scatter(grad.reshape((4,) + grad.shape[2:]), ('section', 'y'), s...]
    ppermute x4 -> x127, waiting for transfers between devices: 6.41 us -> 242 us  [the longest x123 229 us: across(): return lax.ppermute(value, axis, [(i, i ^ bits) for i in range(count)])]
    psum x3 -> x0, waiting for transfers between devices: 162 us -> none  [the longest x2 145 us: shards(): lax.psum(grad_norm_two.astype(jnp.bfloat16), 'tensor').astype(jnp.float32)]
    pallas_call x0 -> x35, Pallas kernels: none -> 144 us  [the longest x32 119 us: call(): pl.pallas_call(body, out_shape=[jax.ShapeDtypeStruct(shape, dtype) for sh...]
    ppermute x4 -> x127, starting transfers between devices: 5.87 us -> 148 us  [the longest x123 140 us: across(): return lax.ppermute(value, axis, [(i, i ^ bits) for i in range(count)])]
    reduce_sum x33 -> x0, other arithmetic: 53.5 us -> none  [the longest x3 14.2 us: shards(): jnp.sum(whole_one * backward_normed_one, axis=0)]
  transfers between devices with their start and end apart: 45 -> 129, of which waited for: 40 -> 48; matrix products, arithmetic and copies ran while one was open for 27% -> 6% of each run, Pallas kernels for 0% -> 18%
where the time goes in v1:
time: 653 us; the launch traced here: 645 us
  waiting for transfers between devices  242 us (37%)
  starting transfers between devices  148 us (23%)
  Pallas kernels  144 us (22%)
  local copies, waits for them, and re-layouts  72.3 us (11%)
  other arithmetic  22.4 us (3%)
  between operations  16.2 us (2%)
    ppermute x123, waiting for transfers between devices, across(): return lax.ppermute(value, axis, [(i, i ^ bits) for i in range(count)])  229 us
    ppermute x123, starting transfers between devices, across(): return lax.ppermute(value, axis, [(i, i ^ bits) for i in range(count)])  140 us
    pallas_call x32, Pallas kernels, call(): pl.pallas_call(body, out_shape=[jax.ShapeDtypeStruct(shape, dtype) for sh...  119 us
    unnamed x379, local copies, waits for them, and re-layouts  52.5 us
    pallas_call x3, Pallas kernels, outer(): pl.pallas_call(body, grid=(4,), out_shape=outs, in_specs=[SMEM] + [pl.Blo...  24.3 us
    ppermute x4, waiting for transfers between devices, routed(): return lax.ppermute(value, AXES, pairs)  13.1 us
  transfers between devices with their start and end apart: 129, of which 48 were waited for; matrix products, arithmetic and copies ran while one was open for 6% of the time, Pallas kernels for 18%

profile of v1, /device:TPU:0, one launch (start us, length us, event | category | flops | bytes accessed | tf_op | source)
XLA Modules:
  0.0 645.0 jit_solution(15433676048365059913)
XLA Ops:
  40.9 6.5 %collective-permute-done.6.refs_5_ = bf16[256,512]{1,0:T(8,128)(2,1)S(1)} collective-permute-done((bf16[256,512]{1,0:T(8,128)(2,1)S(1)}, bf16[256,512]{1,0:T(8,128)(2,1)S(1)}, u32[]{:S(2)}, u32[]{:S(2)}) %collective-permute-start.6) | collective-permute-done | bytes 262176 | tf_op jit(solution)/shard_map/ppermute | solution.py:512
  52.2 8.2 %collective-permute-done.8.refs_2_ = bf16[256,512]{1,0:T(8,128)(2,1)} collective-permute-done((bf16[256,512]{1,0:T(8,128)(2,1)S(1)}, bf16[256,512]{1,0:T(8,128)(2,1)}, u32[]{:S(2)}, u32[]{:S(2)}) %collective-permute-start.8) | collective-permute-done | bytes 262176 | tf_op jit(solution)/shard_map/ppermute | solution.py:512
  71.5 12.8 %collective-permute-done.12.refs_7_ = bf16[256,512]{1,0:T(8,128)(2,1)} collective-permute-done((bf16[256,512]{1,0:T(8,128)(2,1)S(1)}, bf16[256,512]{1,0:T(8,128)(2,1)}, u32[]{:S(2)}, u32[]{:S(2)}) %collective-permute-start.12) | collective-permute-done | bytes 262176 | tf_op jit(solution)/shard_map/ppermute | solution.py:512
  93.2 9.2 %norm_qkv.2 = (bf16[512,2048]{1,0:T(8,128)(2,1)}, bf16[512,2048]{1,0:T(8,128)(2,1)}, bf16[512,2048]{1,0:T(8,128)(2,1)}, bf16[512,256]{1,0:T(8,128)(2,1)S(1)}, bf...) custom-call(s32[4]{0:T(128)S(1)} %pad_add_fusion.2.idx, ...), custom_call_target="tpu_custom_call" | custom-call | flops 1 | bytes 1 | tf_op jit(solution)/shard_map/norm_qkv/pallas_call | solution.py:548
  114.0 8.5 %up_gelu.2 = (bf16[512,1024]{1,0:T(8,128)(2,1)S(1)}, f32[512,1024]{1,0:T(8,128)}) custom-call(s32[4]{0:T(128)S(1)} %pad_add_fusion.2.idx, bf16[1024,256]{1,0:T(8,128)(2,1)S(1)} %get-tuple-element.147.refs_0_.refs_8_, bf16[1024,256]{1,0:T(8,128)(2,1)} %collective-permute-done.7.refs_1_.refs_9_, bf16[1024,256]{1,0:T(8,128)(2,1)} %collective-permute-done.23.refs_2_.refs_10_, ...), custom_call_target="tpu_custom_call" | custom-call | flops 1 | bytes 1 | tf_op jit(solution)/shard_map/up_gelu/pallas_call | solution.py:548
  133.8 11.1 %collective-permute-done.30.refs_3_.refs_11_ = bf16[1280,256]{1,0:T(8,128)(2,1)S(1)} collective-permute-done((bf16[1280,256]{1,0:T(8,128)(2,1)}, bf16[1280,256]{1,0:T(8,128)(2,1)S(1)}, u32[]{:S(2)}, u32[]{:S(2)}) %collective-permute-start.30) | collective-permute-done | bytes 655392 | tf_op jit(solution)/shard_map/ppermute | solution.py:512
  148.4 9.1 %collective-permute-done.68.refs_3_ = bf16[256,512]{1,0:T(8,128)(2,1)} collective-permute-done((bf16[256,512]{1,0:T(8,128)(2,1)}, bf16[256,512]{1,0:T(8,128)(2,1)}, u32[]{:S(2)}, u32[]{:S(2)}) %collective-permute-start.68) | collective-permute-done | bytes 262176 | tf_op jit(solution)/shard_map/ppermute | solution.py:512
  159.6 6.1 collective-permute-start.67
  172.8 6.6 %out_down.2 = (bf16[256,512]{1,0:T(8,128)(2,1)S(1)}, bf16[256,512]{1,0:T(8,128)(2,1)S(1)}, bf16[256,512]{1,0:T(8,128)(2,1)S(1)}, bf16[256,512]{1,0:T(8,128)(2,1)...) custom-call(s32[4]{0:T(128)S(1)} %pad_add_fusion.2.idx, ...), custom_call_target="tpu_custom_call" | custom-call | flops 1 | bytes 1 | tf_op jit(solution)/shard_map/out_down/pallas_call | solution.py:548
  182.1 6.6 %collective-permute-done.37.got = bf16[256,512]{1,0:T(8,128)(2,1)S(1)} collective-permute-done((bf16[256,512]{1,0:T(8,128)(2,1)S(1)}, bf16[256,512]{1,0:T(8,128)(2,1)S(1)}, u32[]{:S(2)}, u32[]{:S(2)}) %collective-permute-start.37) | collective-permute-done | bytes 262176 | tf_op jit(solution)/shard_map/ppermute | solution.py:512
  205.3 7.6 %collective-permute-done.38 = bf16[256,512]{1,0:T(8,128)(2,1)S(1)} collective-permute-done((bf16[256,512]{1,0:T(8,128)(2,1)S(1)}, bf16[256,512]{1,0:T(8,128)(2,1)S(1)}, u32[]{:S(2)}, u32[]{:S(2)}) %collective-permute-start.38) | collective-permute-done | bytes 262176 | tf_op jit(solution)/shard_map/ppermute | solution.py:512
  222.3 8.1 %collective-permute-done.52.refs_3_.refs_11_ = bf16[1024,256]{1,0:T(8,128)(2,1)S(1)} collective-permute-done((bf16[1024,256]{1,0:T(8,128)(2,1)S(1)}, bf16[1024,256]{1,0:T(8,128)(2,1)S(1)}, u32[]{:S(2)}, u32[]{:S(2)}) %collective-permute-start.52) | collective-permute-done | bytes 524320 | tf_op jit(solution)/shard_map/ppermute | solution.py:512
  232.8 7.6 %collective-permute-done.58.refs_2_ = bf16[256,512]{1,0:T(8,128)(2,1)S(1)} collective-permute-done((bf16[256,512]{1,0:T(8,128)(2,1)S(1)}, bf16[256,512]{1,0:T(8,128)(2,1)S(1)}, u32[]{:S(2)}, u32[]{:S(2)}) %collective-permute-start.58) | collective-permute-done | bytes 262176 | tf_op jit(solution)/shard_map/ppermute | solution.py:512
  255.4 9.8 %norm_qkv.3 = (bf16[512,2048]{1,0:T(8,128)(2,1)}, bf16[512,2048]{1,0:T(8,128)(2,1)}, bf16[512,2048]{1,0:T(8,128)(2,1)}, bf16[512,256]{1,0:T(8,128)(2,1)S(1)}, bf...) custom-call(s32[4]{0:T(128)S(1)} %pad_add_fusion.2.idx, ...), custom_call_target="tpu_custom_call" | custom-call | flops 1 | bytes 1 | tf_op jit(solution)/shard_map/norm_qkv/pallas_call | solution.py:548
  270.7 7.6 %up_gelu.3 = (bf16[512,1024]{1,0:T(8,128)(2,1)S(1)}, f32[512,1024]{1,0:T(8,128)}) custom-call(s32[4]{0:T(128)S(1)} %pad_add_fusion.2.idx, bf16[1024,256]{1,0:T(8,128)(2,1)S(1)} %get-tuple-element.168.refs_0_.refs_8_, bf16[1024,256]{1,0:T(8,128)(2,1)S(1)} %collective-permute-done.50.refs_1_.refs_9_, ...), custom_call_target="tpu_custom_call" | custom-call | flops 1 | bytes 1 | tf_op jit(solution)/shard_map/up_gelu/pallas_call | solution.py:548
  283.9 6.6 %out_down.3 = (bf16[256,512]{1,0:T(8,128)(2,1)S(1)}, bf16[256,512]{1,0:T(8,128)(2,1)S(1)}, bf16[256,512]{1,0:T(8,128)(2,1)S(1)}, bf16[256,512]{1,0:T(8,128)(2,1)...) custom-call(s32[4]{0:T(128)S(1)} %pad_add_fusion.2.idx, ...), custom_call_target="tpu_custom_call" | custom-call | flops 1 | bytes 1 | tf_op jit(solution)/shard_map/out_down/pallas_call | solution.py:548
  297.1 8.1 %last_grad.1 = (bf16[512,2048]{1,0:T(8,128)(2,1)}, bf16[512,256]{1,0:T(8,128)(2,1)S(1)}, bf16[512,1024]{1,0:T(8,128)(2,1)}, f32[1,2048]{1,0:T(1,128)S(1)}, f32[1,1024]{1,0:T(1,128)S(1)}) custom-call(s32[4]{0:T(128)S(1)} %pad_add_fusion.2.idx, bf16[256,512]{1,0:T(8,128)(2,1)} %collective-permute-done.65.refs_0_, ...), custom_call_target="tpu_custom_call" | custom-call | flops 1 | bytes 1 | tf_op jit(solution)/shard_map/last_grad/pallas_call | solution.py:548
  313.8 9.1 %outer_uo.1 = bf16[2,2,2,2304,256]{4,3,2,1,0:T(8,128)(2,1)} custom-call(s32[4]{0:T(128)S(1)} %pad_add_fusion.2.idx, bf16[512,2048]{1,0:T(8,128)(2,1)S(1)} %copy-done.2, bf16[512,1024]{1,0:T(8,128)(2,1)S(1)} %copy-done.9, bf16[512,256]{1,0:T(8,128)(2,1)S(1)} %get-tuple-element.182.refs_8_.attn, bf16[512,1024]{1,0:T(8,128)(2,1)S(1)} %copy-done.8, ...), custom_call_target="tpu_custom_call" | custom-call | flops 1 | bytes 1 | tf_op jit(solution)/shard_map/outer_uo/pallas_call | solution.py:926
  334.9 12.0 %grad_mix.2 = (bf16[512,768]{1,0:T(8,128)(2,1)}, f32[1,768]{1,0:T(1,128)S(1)}, f32[4,2048]{1,0:T(4,128)S(1)}, f32[8,512]{1,0:T(8,128)}, bf16[256,512]{1,0:T(8,12...) custom-call(s32[4]{0:T(128)S(1)} %pad_add_fusion.2.idx, ...), custom_call_target="tpu_custom_call" | custom-call | flops 1 | bytes 1 | tf_op jit(solution)/shard_map/grad_mix/pallas_call | solution.py:548
  362.2 5.7 collective-permute-start.87
  377.2 7.5 %collective-permute-done.87 = bf16[256,512]{1,0:T(8,128)(2,1)S(1)} collective-permute-done((bf16[256,512]{1,0:T(8,128)(2,1)S(1)}, bf16[256,512]{1,0:T(8,128)(2,1)S(1)}, u32[]{:S(2)}, u32[]{:S(2)}) %collective-permute-start.87) | collective-permute-done | bytes 262176 | tf_op jit(solution)/shard_map/ppermute | solution.py:512
  394.3 6.3 collective-permute-done.92.refs_1_
  402.3 8.6 %collective-permute-done.93.refs_2_ = bf16[256,512]{1,0:T(8,128)(2,1)S(1)} collective-permute-done((bf16[256,512]{1,0:T(8,128)(2,1)S(1)}, bf16[256,512]{1,0:T(8,128)(2,1)S(1)}, u32[]{:S(2)}, u32[]{:S(2)}) %collective-permute-start.93) | collective-permute-done | bytes 262176 | tf_op jit(solution)/shard_map/ppermute | solution.py:512
  420.2 11.0 %next_grad.1 = (bf16[512,2048]{1,0:T(8,128)(2,1)}, bf16[256,512]{1,0:T(8,128)(2,1)S(1)}, bf16[512,256]{1,0:T(8,128)(2,1)S(1)}, bf16[512,1024]{1,0:T(8,128)(2,1)}...) custom-call(s32[4]{0:T(128)S(1)} %pad_add_fusion.2.idx, bf16[256,512]{1,0:T(8,128)(2,1)S(1)} %add_convert_fusion.2.refs_0_, ...), custom_call_target="tpu_custom_call" | custom-call | flops 1 | bytes 1 | tf_op jit(solution)/shard_map/next_grad/pallas_call | solution.py:548
  435.0 11.5 %outer_all.1 = bf16[2,2,2,3072,256]{4,3,2,1,0:T(8,128)(2,1)} custom-call(s32[4]{0:T(128)S(1)} %pad_add_fusion.2.idx, bf16[512,2048]{1,0:T(8,128)(2,1)S(1)} %copy-done.19, bf16[512,768]{1,0:T(8,128)(2,1)S(1)} %copy-done.81, bf16[512,2048]{1,0:T(8,128)(2,1)} %get-tuple-element.150.refs_8_.refs_0_, bf16[512,1024]{1,0:T(8,128)(2,1)S(1)} %copy-done.10, ...), custom_call_target="tpu_custom_call" | custom-call | flops 1 | bytes 1 | tf_op jit(solution)/shard_map/outer_all/pallas_call | solution.py:926
  457.5 14.3 %grad_mix.3 = (bf16[512,768]{1,0:T(8,128)(2,1)}, f32[1,768]{1,0:T(1,128)S(1)}, f32[4,2048]{1,0:T(4,128)S(1)}, f32[8,512]{1,0:T(8,128)S(1)}, bf16[256,512]{1,0:T(...) custom-call(s32[4]{0:T(128)S(1)} %pad_add_fusion.2.idx, ...), custom_call_target="tpu_custom_call" | custom-call | flops 1 | bytes 1 | tf_op jit(solution)/shard_map/grad_mix/pallas_call | solution.py:548
  482.3 5.6 collective-permute-done.103.got
  513.1 7.0 %collective-permute-done.104.far_b = bf16[256,512]{1,0:T(8,128)(2,1)S(1)} collective-permute-done((bf16[256,512]{1,0:T(8,128)(2,1)S(1)}, bf16[256,512]{1,0:T(8,128)(2,1)S(1)}, u32[]{:S(2)}, u32[]{:S(2)}) %collective-permute-start.104) | collective-permute-done | bytes 262176 | tf_op jit(solution)/shard_map/ppermute | solution.py:512
  520.1 8.8 %collective-permute-done.102.far_a = bf16[256,512]{1,0:T(8,128)(2,1)S(1)} collective-permute-done((bf16[256,512]{1,0:T(8,128)(2,1)S(1)}, bf16[256,512]{1,0:T(8,128)(2,1)S(1)}, u32[]{:S(2)}, u32[]{:S(2)}) %collective-permute-start.102) | collective-permute-done | bytes 262176 | tf_op jit(solution)/shard_map/ppermute | solution.py:512
  587.4 13.1 %collective-permute-done.121 = bf16[2,256,512]{2,1,0:T(8,128)(2,1)S(1)} collective-permute-done((bf16[2,256,512]{2,1,0:T(8,128)(2,1)S(1)}, bf16[2,256,512]{2,1,0:T(8,128)(2,1)S(1)}, u32[]{:S(2)}, u32[]{:S(2)}) %collective-permute-start.121) | collective-permute-done | bytes 524320 | tf_op jit(solution)/shard_map/ppermute | solution.py:532
  619.6 5.9 collective-permute-done.123
  631.1 6.0 unpack_uo.1
  (721 shorter events, 356.3 us)
Async XLA Ops:
  7.2 439.3 %reduce-scatter.3.cloned.1.call-start = ((), (), s32[]{:S(2)}) async-start(), calls=%async_computation.2 | async-start | bytes 11796480 | tf_op jit(solution)/shard_map/reduce_scatter | solution.py:1282
  19.2 28.5 %collective-permute-start.2 = (bf16[2,1024,256]{2,1,0:T(8,128)(2,1)}, bf16[2,1024,256]{2,1,0:T(8,128)(2,1)}, u32[]{:S(2)}, u32[]{:S(2)}) collective-permute-start(bf16[2,1024,256]{2,1,0:T(8,128)(2,1)} %get-tuple-element.141), channel_id=1, source_target_pairs={{0,16},{16,0},{1,17},{17,1},{2,18},{18,2},{3,19},{19,3},{4,20},{20... | collective-permute-start | bytes 3145736 | tf_op jit(solution)/shard_map/ppermute | solution.py:512
  23.5 64.7 %collective-permute-start.1 = (bf16[2,1280,256]{2,1,0:T(8,128)(2,1)}, bf16[2,1280,256]{2,1,0:T(8,128)(2,1)}, u32[]{:S(2)}, u32[]{:S(2)}) collective-permute-start(bf16[2,1280,256]{2,1,0:T(8,128)(2,1)} %get-tuple-element.139), channel_id=1, source_target_pairs={{0,16},{16,0},{1,17},{17,1},{2,18},{18,2},{3,19},{19,3},{4,20},{20... | collective-permute-start | bytes 3932168 | tf_op jit(solution)/shard_map/ppermute | solution.py:512
  61.3 22.9 %collective-permute-start.14 = (bf16[768,256]{1,0:T(8,128)(2,1)S(1)}, bf16[768,256]{1,0:T(8,128)(2,1)}, u32[]{:S(2)}, u32[]{:S(2)}) collective-permute-start(bf16[768,256]{1,0:T(8,128)(2,1)S(1)} %collective-permute-done.4.refs_9_.refs_1_), channel_id=1, source_target_pairs={{0,8},{8,0},{1,9},{9,1},{2,10},{10,2},{3,11},{11,3},{4,12},{12,4},... | collective-permute-start | bytes 1179656 | tf_op jit(solution)/shard_map/ppermute | solution.py:512
  63.1 22.3 %collective-permute-start.7 = (bf16[1024,256]{1,0:T(8,128)(2,1)}, bf16[1024,256]{1,0:T(8,128)(2,1)}, u32[]{:S(2)}, u32[]{:S(2)}) collective-permute-start(bf16[1024,256]{1,0:T(8,128)(2,1)} %get-tuple-element.144), channel_id=1, source_target_pairs={{0,4},{4,0},{1,5},{5,1},{2,6},{6,2},{3,7},{7,3},{8,12},{12,8},{9,1... | collective-permute-start | bytes 1572872 | tf_op jit(solution)/shard_map/ppermute | solution.py:512
  88.8 23.8 %collective-permute-start.28 = (bf16[1024,256]{1,0:T(8,128)(2,1)}, bf16[1024,256]{1,0:T(8,128)(2,1)}, u32[]{:S(2)}, u32[]{:S(2)}) collective-permute-start(bf16[1024,256]{1,0:T(8,128)(2,1)} %collective-permute-done.23.refs_2_.refs_10_), channel_id=1, source_target_pairs={{0,16},{16,0},{1,17},{17,1},{2,18},{18,2},{3,19},{19,3},{4,20},{20... | collective-permute-start | bytes 1572872 | tf_op jit(solution)/shard_map/ppermute | solution.py:512
  130.8 28.8 %collective-permute-start.33 = (bf16[1280,256]{1,0:T(8,128)(2,1)S(1)}, bf16[1280,256]{1,0:T(8,128)(2,1)S(1)}, u32[]{:S(2)}, u32[]{:S(2)}) collective-permute-start(bf16[1280,256]{1,0:T(8,128)(2,1)S(1)} %collective-permute-done.24.refs_2_.refs_10_), channel_id=1, source_target_pairs={{0,16},{16,0},{1,17},{17,1},{2,18},{18,2},{3,19},{19,3},{4,20},{20... | collective-permute-start | bytes 1966088 | tf_op jit(solution)/shard_map/ppermute | solution.py:512
  133.8 31.9 %collective-permute-start.32 = (bf16[1280,256]{1,0:T(8,128)(2,1)}, bf16[1280,256]{1,0:T(8,128)(2,1)S(1)}, u32[]{:S(2)}, u32[]{:S(2)}) collective-permute-start(bf16[1280,256]{1,0:T(8,128)(2,1)} %collective-permute-done.22.refs_1_.refs_9_), channel_id=1, source_target_pairs={{0,16},{16,0},{1,17},{17,1},{2,18},{18,2},{3,19},{19,3},{4,20},{20... | collective-permute-start | bytes 1966088 | tf_op jit(solution)/shard_map/ppermute | solution.py:512
  144.9 22.7 %collective-permute-start.34 = (bf16[1280,256]{1,0:T(8,128)(2,1)S(1)}, bf16[1280,256]{1,0:T(8,128)(2,1)S(1)}, u32[]{:S(2)}, u32[]{:S(2)}) collective-permute-start(bf16[1280,256]{1,0:T(8,128)(2,1)S(1)} %collective-permute-done.30.refs_3_.refs_11_), channel_id=1, source_target_pairs={{0,16},{16,0},{1,17},{17,1},{2,18},{18,2},{3,19},{19,3},{4,20},{20... | collective-permute-start | bytes 1966088 | tf_op jit(solution)/shard_map/ppermute | solution.py:512
  157.5 24.1 %collective-permute-start.50 = (bf16[1024,256]{1,0:T(8,128)(2,1)}, bf16[1024,256]{1,0:T(8,128)(2,1)S(1)}, u32[]{:S(2)}, u32[]{:S(2)}) collective-permute-start(bf16[1024,256]{1,0:T(8,128)(2,1)} %get-tuple-element.167), channel_id=1, source_target_pairs={{0,4},{4,0},{1,5},{5,1},{2,6},{6,2},{3,7},{7,3},{8,12},{12,8},{9,1... | collective-permute-start | bytes 1572872 | tf_op jit(solution)/shard_map/ppermute | solution.py:512
  159.5 22.0 %collective-permute-start.44 = (bf16[768,256]{1,0:T(8,128)(2,1)}, bf16[768,256]{1,0:T(8,128)(2,1)S(1)}, u32[]{:S(2)}, u32[]{:S(2)}) collective-permute-start(bf16[768,256]{1,0:T(8,128)(2,1)} %get-tuple-element.165.refs_8_.refs_0_), channel_id=1, source_target_pairs={{0,8},{8,0},{1,9},{9,1},{2,10},{10,2},{3,11},{11,3},{4,12},{12,4},... | collective-permute-start | bytes 1179656 | tf_op jit(solution)/shard_map/ppermute | solution.py:512
  181.6 23.2 %collective-permute-start.47 = (bf16[768,256]{1,0:T(8,128)(2,1)S(1)}, bf16[768,256]{1,0:T(8,128)(2,1)S(1)}, u32[]{:S(2)}, u32[]{:S(2)}) collective-permute-start(bf16[768,256]{1,0:T(8,128)(2,1)S(1)} %collective-permute-done.43.refs_9_.refs_1_), channel_id=1, source_target_pairs={{0,16},{16,0},{1,17},{17,1},{2,18},{18,2},{3,19},{19,3},{4,20},{20... | collective-permute-start | bytes 1179656 | tf_op jit(solution)/shard_map/ppermute | solution.py:512
  181.6 23.2 %collective-permute-start.48 = (bf16[768,256]{1,0:T(8,128)(2,1)S(1)}, bf16[768,256]{1,0:T(8,128)(2,1)S(1)}, u32[]{:S(2)}, u32[]{:S(2)}) collective-permute-start(bf16[768,256]{1,0:T(8,128)(2,1)S(1)} %collective-permute-done.44.refs_10_.refs_2_), channel_id=1, source_target_pairs={{0,16},{16,0},{1,17},{17,1},{2,18},{18,2},{3,19},{19,3},{4,20},{20... | collective-permute-start | bytes 1179656 | tf_op jit(solution)/shard_map/ppermute | solution.py:512
  240.4 26.1 %collective-permute-start.75 = (bf16[1280,256]{1,0:T(8,128)(2,1)S(1)}, bf16[1280,256]{1,0:T(8,128)(2,1)S(1)}, u32[]{:S(2)}, u32[]{:S(2)}) collective-permute-start(bf16[1280,256]{1,0:T(8,128)(2,1)S(1)} %collective-permute-done.73.refs_1_.refs_9_), channel_id=1, source_target_pairs={{0,8},{8,0},{1,9},{9,1},{2,10},{10,2},{3,11},{11,3},{4,12},{12,4},... | collective-permute-start | bytes 1966088 | tf_op jit(solution)/shard_map/ppermute | solution.py:512
  241.0 25.0 %collective-permute-start.55 = (bf16[1024,256]{1,0:T(8,128)(2,1)S(1)}, bf16[1024,256]{1,0:T(8,128)(2,1)S(1)}, u32[]{:S(2)}, u32[]{:S(2)}) collective-permute-start(bf16[1024,256]{1,0:T(8,128)(2,1)S(1)} %collective-permute-done.51.refs_2_.refs_10_), channel_id=1, source_target_pairs={{0,16},{16,0},{1,17},{17,1},{2,18},{18,2},{3,19},{19,3},{4,20},{20... | collective-permute-start | bytes 1572872 | tf_op jit(solution)/shard_map/ppermute | solution.py:512
  266.6 25.4 %collective-permute-start.72 = (bf16[256,512]{1,0:T(8,128)(2,1)}, bf16[256,512]{1,0:T(8,128)(2,1)S(1)}, u32[]{:S(2)}, u32[]{:S(2)}) collective-permute-start(bf16[256,512]{1,0:T(8,128)(2,1)} %collective-permute-done.68.refs_3_), channel_id=1, source_target_pairs={{0,4},{4,0},{1,5},{5,1},{2,6},{6,2},{3,7},{7,3},{8,12},{12,8},{9,1... | collective-permute-start | bytes 786440 | tf_op jit(solution)/shard_map/ppermute | solution.py:512
  268.2 24.6 %collective-permute-start.71 = (bf16[256,512]{1,0:T(8,128)(2,1)}, bf16[256,512]{1,0:T(8,128)(2,1)S(1)}, u32[]{:S(2)}, u32[]{:S(2)}) collective-permute-start(bf16[256,512]{1,0:T(8,128)(2,1)} %collective-permute-done.67.refs_2_), channel_id=1, source_target_pairs={{0,4},{4,0},{1,5},{5,1},{2,6},{6,2},{3,7},{7,3},{8,12},{12,8},{9,1... | collective-permute-start | bytes 786440 | tf_op jit(solution)/shard_map/ppermute | solution.py:512
  268.7 24.8 %collective-permute-start.70 = (bf16[256,512]{1,0:T(8,128)(2,1)}, bf16[256,512]{1,0:T(8,128)(2,1)S(1)}, u32[]{:S(2)}, u32[]{:S(2)}) collective-permute-start(bf16[256,512]{1,0:T(8,128)(2,1)} %collective-permute-done.66.refs_1_), channel_id=1, source_target_pairs={{0,4},{4,0},{1,5},{5,1},{2,6},{6,2},{3,7},{7,3},{8,12},{12,8},{9,1... | collective-permute-start | bytes 786440 | tf_op jit(solution)/shard_map/ppermute | solution.py:512
  270.2 23.2 %collective-permute-start.69 = (bf16[256,512]{1,0:T(8,128)(2,1)}, bf16[256,512]{1,0:T(8,128)(2,1)S(1)}, u32[]{:S(2)}, u32[]{:S(2)}) collective-permute-start(bf16[256,512]{1,0:T(8,128)(2,1)} %collective-permute-done.65.refs_0_), channel_id=1, source_target_pairs={{0,4},{4,0},{1,5},{5,1},{2,6},{6,2},{3,7},{7,3},{8,12},{12,8},{9,1... | collective-permute-start | bytes 786440 | tf_op jit(solution)/shard_map/ppermute | solution.py:512
  308.5 25.6 %collective-permute-start.84 = (bf16[512,512]{1,0:T(8,128)(2,1)S(1)}, bf16[512,512]{1,0:T(8,128)(2,1)S(1)}, u32[]{:S(2)}, u32[]{:S(2)}) collective-permute-start(bf16[512,512]{1,0:T(8,128)(2,1)S(1)} %get-tuple-element.197), channel_id=1, source_target_pairs={{0,16},{16,0},{1,17},{17,1},{2,18},{18,2},{3,19},{19,3},{4,20},{20... | collective-permute-start | bytes 1572872 | tf_op jit(solution)/shard_map/ppermute | solution.py:512
  312.1 21.9 %collective-permute-start.83 = (bf16[256,512]{1,0:T(8,128)(2,1)S(1)}, bf16[256,512]{1,0:T(8,128)(2,1)S(1)}, u32[]{:S(2)}, u32[]{:S(2)}) collective-permute-start(bf16[256,512]{1,0:T(8,128)(2,1)S(1)} %get-tuple-element.194), channel_id=1, source_target_pairs={{0,4},{4,0},{1,5},{5,1},{2,6},{6,2},{3,7},{7,3},{8,12},{12,8},{9,1... | collective-permute-start | bytes 786440 | tf_op jit(solution)/shard_map/ppermute | solution.py:512
  351.2 206.8 %reduce-scatter.5.cloned.1.call-start = ((), (), s32[]{:S(2)}) async-start(), calls=%async_computation.3 | async-start | bytes 15728640 | tf_op jit(solution)/shard_map/reduce_scatter | solution.py:1282
  355.1 22.1 %collective-permute-start.85 = (bf16[256,512]{1,0:T(8,128)(2,1)}, bf16[256,512]{1,0:T(8,128)(2,1)S(1)}, u32[]{:S(2)}, u32[]{:S(2)}) collective-permute-start(bf16[256,512]{1,0:T(8,128)(2,1)} %copy-done.156), channel_id=1, source_target_pairs={{0,4},{4,0},{1,5},{5,1},{2,6},{6,2},{3,7},{7,3},{8,12},{12,8},{9,1... | collective-permute-start | bytes 786440 | tf_op jit(solution)/shard_map/ppermute | solution.py:512
  362.2 22.5 %collective-permute-start.87 = (bf16[256,512]{1,0:T(8,128)(2,1)S(1)}, bf16[256,512]{1,0:T(8,128)(2,1)S(1)}, u32[]{:S(2)}, u32[]{:S(2)}) collective-permute-start(bf16[256,512]{1,0:T(8,128)(2,1)S(1)} %add_piece.15), channel_id=1, source_target_pairs={{0,2},{1,3},{2,0},{3,1},{4,6},{5,7},{6,4},{7,5},{8,10},{9,11},{10,... | collective-permute-start | bytes 786440 | tf_op jit(solution)/shard_map/ppermute | solution.py:512
  390.7 21.6 %collective-permute-start.94 = (bf16[256,512]{1,0:T(8,128)(2,1)S(1)}, bf16[256,512]{1,0:T(8,128)(2,1)S(1)}, u32[]{:S(2)}, u32[]{:S(2)}) collective-permute-start(bf16[256,512]{1,0:T(8,128)(2,1)S(1)} %add_convert_fusion.2.refs_0_), channel_id=1, source_target_pairs={{0,3},{1,2},{2,1},{3,0},{4,7},{5,6},{6,5},{7,4},{8,11},{9,10},{10,... | collective-permute-start | bytes 786440 | tf_op jit(solution)/shard_map/ppermute | solution.py:512
  476.8 21.7 %collective-permute-start.100 = (bf16[256,512]{1,0:T(8,128)(2,1)S(1)}, bf16[256,512]{1,0:T(8,128)(2,1)S(1)}, u32[]{:S(2)}, u32[]{:S(2)}) collective-permute-start(bf16[256,512]{1,0:T(8,128)(2,1)S(1)} %get-tuple-element.220), channel_id=1, source_target_pairs={{0,4},{4,0},{1,5},{5,1},{2,6},{6,2},{3,7},{7,3},{8,12},{12,8},{9,1... | collective-permute-start | bytes 786440 | tf_op jit(solution)/shard_map/ppermute | solution.py:512
  501.4 27.5 %collective-permute-start.116 = (bf16[2304,256]{1,0:T(8,128)(2,1)S(1)}, bf16[2304,256]{1,0:T(8,128)(2,1)S(1)}, u32[]{:S(2)}, u32[]{:S(2)}) collective-permute-start(bf16[2304,256]{1,0:T(8,128)(2,1)S(1)} %get-tuple-element.309), channel_id=1, source_target_pairs={{0,4},{4,0},{1,5},{5,1},{2,6},{6,2},{3,7},{7,3},{8,12},{12,8},{9,1... | collective-permute-start | bytes 3538952 | tf_op jit(solution)/shard_map/ppermute | solution.py:512
  507.4 21.5 %collective-permute-start.102 = (bf16[256,512]{1,0:T(8,128)(2,1)S(1)}, bf16[256,512]{1,0:T(8,128)(2,1)S(1)}, u32[]{:S(2)}, u32[]{:S(2)}) collective-permute-start(bf16[256,512]{1,0:T(8,128)(2,1)S(1)} %add_piece.18), channel_id=1, source_target_pairs={{0,2},{1,3},{2,0},{3,1},{4,6},{5,7},{6,4},{7,5},{8,10},{9,11},{10,... | collective-permute-start | bytes 786440 | tf_op jit(solution)/shard_map/ppermute | solution.py:512
  532.7 23.0 %collective-permute-start.117 = (bf16[4,768,256]{2,1,0:T(8,128)(2,1)}, bf16[4,768,256]{2,1,0:T(8,128)(2,1)}, u32[]{:S(2)}, u32[]{:S(2)}) collective-permute-start(bf16[4,768,256]{2,1,0:T(8,128)(2,1)} %get-tuple-element.253), channel_id=1, source_target_pairs={{0,16},{16,0},{1,17},{17,1},{2,18},{18,2},{3,19},{19,3},{4,20},{20... | collective-permute-start | bytes 4718600 | tf_op jit(solution)/shard_map/ppermute | solution.py:512
  557.0 21.4 %collective-permute-start.118 = (bf16[2,768,256]{2,1,0:T(8,128)(2,1)S(1)}, bf16[2,768,256]{2,1,0:T(8,128)(2,1)}, u32[]{:S(2)}, u32[]{:S(2)}) collective-permute-start(bf16[2,768,256]{2,1,0:T(8,128)(2,1)S(1)} %fusion), channel_id=1, source_target_pairs={{0,8},{8,0},{1,9},{9,1},{2,10},{10,2},{3,11},{11,3},{4,12},{12,4},... | collective-permute-start | bytes 2359304 | tf_op jit(solution)/shard_map/ppermute | solution.py:512
  561.9 39.7 %collective-permute-start.124 = (bf16[3072,256]{1,0:T(8,128)(2,1)}, bf16[3072,256]{1,0:T(8,128)(2,1)}, u32[]{:S(2)}, u32[]{:S(2)}) collective-permute-start(bf16[3072,256]{1,0:T(8,128)(2,1)} %get-tuple-element.302), channel_id=1, source_target_pairs={{0,4},{4,0},{1,5},{5,1},{2,6},{6,2},{3,7},{7,3},{8,12},{12,8},{9,1... | collective-permute-start | bytes 4718600 | tf_op jit(solution)/shard_map/ppermute | solution.py:512
  606.6 24.5 %collective-permute-start.126 = (bf16[2,2304,256]{2,1,0:T(8,128)(2,1)}, bf16[2,2304,256]{2,1,0:T(8,128)(2,1)}, u32[]{:S(2)}, u32[]{:S(2)}) collective-permute-start(bf16[2,2304,256]{2,1,0:T(8,128)(2,1)} %get-tuple-element.300), channel_id=1, source_target_pairs={{0,16},{16,0},{1,17},{17,1},{2,18},{18,2},{3,19},{19,3},{4,20},{20... | collective-permute-start | bytes 7077896 | tf_op jit(solution)/shard_map/ppermute | solution.py:512
  (283 other events, 3971.6 us)
Sparse Core Ops, SparseCore 0:
  351.2 80.8 reduce-scatter.2
  446.7 98.1 reduce-scatter.4
